TPU v7x, 128 devices: a whole 4x4x4 slice. The times are simulated.
128 devices in a mesh: grp: 8 (over x, core), head: 16 (over y, z).
Axes of the slice: x: 4, y: 4, z: 4, core: 2. Of those that a mesh axis runs over, the one named last changes fastest.
Arguments:
- query_in: bfloat16 [64, 2, 8192], P('grp', None, 'head'), may hold values from -6 to 6
- key_in: bfloat16 [64, 2, 8192], P('grp', None, 'head'), may hold values from -6 to 6
- value_in: bfloat16 [64, 2, 8192], P('grp', None, 'head'), may hold values from -6 to 6
- decay_rate: float32 [64], P('head'), may hold values from 0.6 to 0.995
- states: float32 [64, 64, 128, 128], P('grp', 'head'), may hold values from -6 to 6
- attn_gain: float32 [8192], P('head'), may hold values from 0.25 to 1.75
- out_proj: bfloat16 [8192, 6144], P('head', 'grp'), may hold values from -0.0625 to 0.0625
- stream_in: bfloat16 [64, 2, 6144], P('head', None, 'grp'), may hold values from -27 to 27
- ffn_gain: float32 [6144], replicated, may hold values from 0.1 to 1.9
- expert_gate: bfloat16 [16, 4608, 6144], P('head', 'grp'), may hold values from -0.078125 to 0.078125
- expert_up: bfloat16 [16, 4608, 6144], P('head', 'grp'), may hold values from -0.078125 to 0.078125
- expert_down: bfloat16 [16, 4608, 6144], P('head', 'grp'), may hold values from -0.09375 to 0.09375
- routes: int32 [64, 2, 2], P('head'), may hold values from 0 to 15, as said below
- route_weights: float32 [64, 2, 2], P('head'), may hold values from 0.2 to 1
Outputs:
- stream_out: bfloat16 [64, 2, 6144], P('head', None, 'grp')
- states_out: float32 [64, 64, 128, 128], P('grp', 'head')
Inputs may be any that keep to these rules, and one draw needn't show every extreme that they name: `routes`: each row names two different experts. Within the 8 token rows of one head index (aligned blocks of 4 requests), no expert is named more than 2 times, and some expert is named exactly 2 times within every such block.
All inputs are finite; a program needn't handle non-finite values.
Results may differ from a plain program's by a relative error of at most 0.0054.
Values may be sent and summed in bfloat16 or wider, within the bound.
No kernel may reach another device: no remote copies, remote signals or barrier semaphores. Data moves between devices by JAX's collectives and lax.ppermute only.
A program may use at most 128 MiB of HBM per device.

v0:
```python
import jax
import jax.numpy as jnp
from jax import lax
from jax.sharding import PartitionSpec as P

CAP = 2


EPSILON = 1e-06


def expert_rows(slot_rows, gate_local, up_local, down_local):
    sources, slots, width = slot_rows.shape
    flattened = slot_rows.reshape(sources * slots, width)
    contract = (((1,), (1,)), ((), ()))
    gate_out = lax.dot_general(flattened, gate_local, contract, preferred_element_type=jnp.float32)
    upward = lax.dot_general(flattened, up_local, contract, preferred_element_type=jnp.float32)
    activated = (jax.nn.silu(gate_out) * upward).astype(jnp.bfloat16)
    produced = jnp.dot(activated, down_local, preferred_element_type=jnp.float32)
    return produced.reshape(sources, slots, down_local.shape[1])


def body(
    query_in,
    key_in,
    value_in,
    decay_rate,
    states,
    attn_gain,
    out_proj,
    stream_in,
    ffn_gain,
    expert_gate,
    expert_up,
    expert_down,
    routes,
    route_weights,
):
    requests_here, positions, width_here = query_in.shape
    head_count = states.shape[1]
    head_size = states.shape[2]
    shape_four = (requests_here, positions, head_count, head_size)
    queries = query_in.astype(jnp.float32).reshape(shape_four)
    keyset = key_in.reshape(shape_four)
    valueset = value_in.reshape(shape_four)
    memory_state = states
    outputs = []
    for position in range(positions):
        outer = jnp.einsum(
            "rhk,rhv->rhkv",
            keyset[:, position],
            valueset[:, position],
            preferred_element_type=jnp.float32,
        )
        memory_state = decay_rate[None, :, None, None] * memory_state + outer
        outputs.append(
            jnp.einsum(
                "rhk,rhkv->rhv", queries[:, position], memory_state, precision=lax.Precision.HIGHEST
            )
        )
    readout = jnp.stack(outputs, axis=1)
    scaled = (
        readout
        * lax.rsqrt(jnp.mean(readout * readout, axis=-1, keepdims=True) + EPSILON)
        * attn_gain.reshape(head_count, head_size)
    )
    attended = scaled.astype(jnp.bfloat16).reshape(requests_here * positions, width_here)
    partial_sums = jnp.dot(
        lax.all_gather(attended, "grp", axis=0, tiled=True),
        out_proj,
        preferred_element_type=jnp.float32,
    )
    mixed = lax.psum_scatter(partial_sums, "head", scatter_dimension=0, tiled=True)
    tokens_here = mixed.shape[0]
    columns = mixed.shape[1]
    model_width = columns * lax.axis_size("grp")
    residual = (stream_in.astype(jnp.float32).reshape(tokens_here, columns) + mixed).astype(
        jnp.bfloat16
    )
    experts = lax.axis_size("head") * expert_gate.shape[0]
    chosen = routes.reshape(tokens_here, 2)
    weighting = route_weights.reshape(tokens_here, 2)
    onehot = (
        (chosen[:, :, None] == jnp.arange(experts, dtype=jnp.int32)[None, None, :])
        .astype(jnp.int32)
        .reshape(tokens_here * 2, experts)
    )
    earlier = jnp.cumsum(onehot, axis=0) - onehot
    slot_index = jnp.sum(earlier * onehot, axis=1).reshape(tokens_here, 2)
    slot_code = chosen * CAP + slot_index
    slots_all = experts * CAP
    selection = (
        jnp.arange(slots_all, dtype=jnp.int32)[:, None, None] == slot_code[None, :, :]
    ).astype(jnp.float32)
    picker = jnp.sum(selection, axis=2).astype(jnp.bfloat16)
    combiner = jnp.transpose(jnp.sum(selection * weighting[None, :, :], axis=2))
    gate_local = expert_gate[0]
    up_local = expert_up[0]
    down_local = expert_down[0]
    full_rows = lax.all_gather(residual, "grp", axis=1, tiled=True).astype(jnp.float32)
    normed = (
        full_rows
        * lax.rsqrt(jnp.mean(full_rows * full_rows, axis=-1, keepdims=True) + EPSILON)
        * ffn_gain
    ).astype(jnp.bfloat16)
    outgoing = (
        jnp.dot(picker, normed, preferred_element_type=jnp.float32)
        .astype(jnp.bfloat16)
        .reshape(experts, CAP, model_width)
    )
    produced = expert_rows(
        lax.all_to_all(outgoing, "head", split_axis=0, concat_axis=0, tiled=True),
        gate_local,
        up_local,
        down_local,
    )
    returned = lax.all_to_all(produced, "head", split_axis=0, concat_axis=0, tiled=True)
    weighted = jnp.dot(
        combiner,
        returned.reshape(slots_all, model_width),
        precision=lax.Precision.HIGHEST,
        preferred_element_type=jnp.float32,
    )
    moe = lax.psum_scatter(weighted, "grp", scatter_dimension=1, tiled=True)
    stream_out = (residual.astype(jnp.float32) + moe).astype(jnp.bfloat16).reshape(stream_in.shape)
    return (stream_out, memory_state)


def solution(mesh):
    return jax.shard_map(
        body,
        mesh=mesh,
        in_specs=(
            P("grp", None, "head"),
            P("grp", None, "head"),
            P("grp", None, "head"),
            P("head"),
            P("grp", "head", None, None),
            P("head"),
            P("head", "grp"),
            P("head", None, "grp"),
            P(),
            P("head", "grp", None),
            P("head", "grp", None),
            P("head", "grp", None),
            P("head", None, None),
            P("head", None, None),
        ),
        out_specs=(P("head", None, "grp"), P("grp", "head", None, None)),
        check_vma=False,
    )
```

profile of v0, /device:TPU:1, one launch (start us, length us, event | category | flops | bytes accessed | tf_op | source)
XLA Modules:
  0.0 215.0 jit_solution(18027664069437284102)
XLA Ops:
  7.2 0.0 copy-start
  7.2 0.0 copy-start.1
  7.2 0.0 copy-start.6
  7.2 0.0 all-reduce.3.cloned.1.call-start
  7.2 0.9 reshape.101
  8.2 0.7 reshape.97
  8.9 0.7 reshape.99
  9.6 2.9 %fusion.6 = f32[8,4,1,128]{3,2,1,0:T(1,128)S(1)} fusion(f32[8,4,128,128]{3,2,1,0:T(8,128)} %param.18, f32[8,4,128]{2,1,0:T(4,128)S(1)} %get-tuple-element.8, f32[8,4,128]{2,1,0:T(4,128)S(1)} %get-tuple-element.11, f32[4]{0:T(128)} %param.17, bf16[8,4,128,1]{2,1,0,3:T(4,128)(2,1)S(1)} %get-tuple-element.4), kind=kOutput, calls=%fused_computation.9 | convolution fusion | flops 7864320 | bytes 2154512 | tf_op jit(solution)/shard_map/rhk,rhkv->rhv/dot_general | solution.py:57
  12.6 0.0 copy-done.1
  12.6 0.0 copy-done.6
  12.6 1.3 multiply_add_fusion
  13.9 0.0 copy-start.2
  13.9 0.0 copy-start.7
  13.9 0.0 copy-start.5
  13.9 1.3 copy-done.2
  15.2 0.0 copy-start.8
  15.2 0.0 copy-start.4
  15.2 0.0 copy-start.9
  15.2 0.0 copy-start.3
  15.2 1.1 fusion.26
  16.3 0.1 multiply_reduce_fusion
  16.4 0.1 fusion.25
  16.5 0.0 copy-done.7
  16.5 14.4 %all_gather.6 = bf16[128,512]{1,0:T(8,128)(2,1)S(1)} all-gather(bf16[16,512]{1,0:T(8,128)(2,1)S(1)} %fusion.23), channel_id=1, replica_groups=mesh['grp'=8,'head'=16] {'grp'}, dimensions={0}, use_global_device_ids=true | all-gather | bytes 147456 | tf_op jit(solution)/shard_map/all_gather | solution.py:69
  31.0 0.0 copy-done
  31.0 1.0 fusion.35
  32.0 0.0 all-reduce.3.cloned.1.call-update
  32.0 0.0 reduce-scatter.2.cloned.1.call-start
  32.1 0.0 copy-done.5
  32.1 0.1 copy.56
  32.2 0.1 copy.55
  32.3 0.1 mul.97
  32.4 0.0 copy-done.8
  32.4 0.1 copy.58
  32.5 0.1 mul.99
  32.6 0.1 eq.30
  32.7 0.1 fusion.33
  32.8 0.2 select_reduce_fusion.1
  33.0 0.1 reshape.104
  33.0 0.1 copy.57
  33.1 0.0 copy-done.4
  33.1 0.0 copy-done.9
  33.2 0.6 dynamic-slice
  34.4 0.1 convert_reduce_fusion
  34.5 82.1 %all-reduce.3.cloned.1.call-done = f32[128,768]{1,0:T(8,128)} async-done(((f32[128,768]{1,0:T(8,128)}), f32[128,768]{1,0:T(8,128)}) %all-reduce.3.cloned.1.call-update) | async-done | bytes 393232
  116.6 0.7 fusion.24
  117.3 14.9 %all_gather.7 = bf16[8,6144]{1,0:T(8,128)(2,1)S(1)} all-gather(bf16[8,768]{1,0:T(8,128)(2,1)S(1)} %fusion.24), channel_id=1, replica_groups=mesh['grp'=8,'head'=16] {'grp'}, dimensions={1}, use_global_device_ids=true | all-gather | bytes 110592 | tf_op jit(solution)/shard_map/all_gather | solution.py:100
  132.2 0.2 fusion.16
  132.4 0.0 copy-done.3
  132.4 0.3 convolution_convert_fusion
  132.7 0.3 reshape.105
  133.0 13.8 %all_to_all.10 = bf16[16,2,6144]{2,1,0:T(2,128)(2,1)S(1)} all-to-all(bf16[16,2,6144]{2,1,0:T(2,128)(2,1)S(1)} %reshape.105), channel_id=1, replica_groups=mesh['grp'=8,'head'=16] {'head'}, dimensions={0} | all-to-all | bytes 786432 | tf_op jit(solution)/shard_map/all_to_all | solution.py:112
  146.7 0.1 reshape.106
  146.9 5.1 %fusion.4 = f32[32,576]{1,0:T(8,128)S(1)} fusion(bf16[32,6144]{1,0:T(8,128)(2,1)S(1)} %reshape.106, bf16[1,576,6144]{2,1,0:T(8,128)(2,1)} %param.23), kind=kOutput, calls=%fused_computation.4 | convolution fusion | flops 226492416 | bytes 7544832 | tf_op jit(solution)/shard_map/dot_general | solution.py:16
  152.0 5.2 %fusion.10 = bf16[32,576]{1,0:T(8,128)(2,1)S(1)} fusion(bf16[32,6144]{1,0:T(8,128)(2,1)S(1)} %reshape.106, bf16[1,576,6144]{2,1,0:T(8,128)(2,1)} %param.24, f32[32,576]{1,0:T(8,128)S(1)} %fusion.4), kind=kOutput, calls=%fused_computation.11 | convolution fusion | flops 226603008 | bytes 7581696 | tf_op jit(solution)/shard_map/dot_general | solution.py:17
  157.2 4.3 %fusion = f32[16,2,6144]{2,0,1:T(8,128)S(1)} fusion(bf16[1,576,6144]{2,1,0:T(8,128)(2,1)} %param.25, bf16[16,2,576]{2,1,0:T(2,128)(2,1)S(1)} %dot_general.52), kind=kOutput, calls=%fused_computation | convolution fusion | flops 226492416 | bytes 7901184 | tf_op jit(solution)/shard_map/dot_general | solution.py:19
  161.5 0.6 copy.60
  162.1 15.1 %all_to_all.11 = f32[16,2,6144]{2,1,0:T(2,128)S(1)} all-to-all(f32[16,2,6144]{2,1,0:T(2,128)S(1)} %copy.60), channel_id=1, replica_groups=mesh['grp'=8,'head'=16] {'head'}, dimensions={0} | all-to-all | bytes 1572864 | tf_op jit(solution)/shard_map/all_to_all | solution.py:117
  177.3 0.5 reshape.107
  177.8 1.2 fusion.36
  179.0 0.0 reduce-scatter.2.cloned.1.call-update
  179.0 27.8 %reduce-scatter.2.cloned.1.call-done = f32[8,768]{1,0:T(8,128)} async-done(((f32[8,6144]{1,0:T(8,128)}), f32[8,768]{1,0:T(8,128)}) %reduce-scatter.2.cloned.1.call-update) | async-done | bytes 24592 | tf_op jit(solution)/shard_map/reduce_scatter | solution.py:124
  206.8 0.7 add_convert_fusion
  207.6 0.6 reshape.108
  (10 shorter events, 0.1 us)
Async XLA Ops:
  7.2 23.8 %copy-start = (bf16[512,768]{1,0:T(8,128)(2,1)S(1)}, bf16[512,768]{1,0:T(8,128)(2,1)}, u32[]{:S(2)}) copy-start(bf16[512,768]{1,0:T(8,128)(2,1)} %param.20) | copy-start | bytes 2359300
  7.2 5.4 %copy-start.1 = (f32[8,4,128,128]{3,2,1,0:T(8,128)S(1)}, f32[8,4,128,128]{3,2,1,0:T(8,128)}, u32[]{:S(2)}) copy-start(f32[8,4,128,128]{3,2,1,0:T(8,128)} %param.18) | copy-start | bytes 6291460
  7.2 5.4 %copy-start.6 = (f32[4]{0:T(128)S(1)}, f32[4]{0:T(128)}, u32[]{:S(2)}) copy-start(f32[4]{0:T(128)} %param.17) | copy-start | bytes 52
  7.2 109.4 %all-reduce.3.cloned.1.call-start = ((), (), s32[]{:S(2)}) async-start(), calls=%async_computation.4 | async-start | bytes 786432
  13.9 1.3 copy-start.2
  13.9 2.6 %copy-start.7 = (f32[512]{0:T(512)S(1)}, f32[512]{0:T(512)}, u32[]{:S(2)}) copy-start(f32[512]{0:T(512)} %param.19) | copy-start | bytes 6148
  13.9 18.2 %copy-start.5 = (s32[4,2,2]{0,2,1:T(2,128)S(1)}, s32[4,2,2]{0,2,1:T(2,128)}, u32[]{:S(2)}) copy-start(s32[4,2,2]{0,2,1:T(2,128)} %param.26) | copy-start | bytes 196
  15.2 17.2 %copy-start.8 = (f32[4,2,2]{0,2,1:T(2,128)S(1)}, f32[4,2,2]{0,2,1:T(2,128)}, u32[]{:S(2)}) copy-start(f32[4,2,2]{0,2,1:T(2,128)} %param.27) | copy-start | bytes 196
  15.2 17.9 %copy-start.4 = (bf16[4,2,768]{2,1,0:T(2,128)(2,1)S(1)}, bf16[4,2,768]{2,1,0:T(2,128)(2,1)}, u32[]{:S(2)}) copy-start(bf16[4,2,768]{2,1,0:T(2,128)(2,1)} %param.21) | copy-start | bytes 36868
  15.2 17.9 %copy-start.9 = (u32[128]{0:T(128)S(1)}, u32[128]{0:T(128)}, u32[]{:S(2)}) copy-start(u32[128]{0:T(128)} %constant.33) | copy-start | bytes 1540
  15.2 117.2 %copy-start.3 = (f32[6144]{0:T(1024)S(1)}, f32[6144]{0:T(1024)}, u32[]{:S(2)}) copy-start(f32[6144]{0:T(1024)} %param.22) | copy-start | bytes 73732
  32.0 174.8 %reduce-scatter.2.cloned.1.call-start = ((), (), s32[]{:S(2)}) async-start(), calls=%async_computation.3 | async-start | bytes 221184 | tf_op jit(solution)/shard_map/reduce_scatter | solution.py:124
Sparse Core Ops, SparseCore 0:
  32.1 84.4 all-reduce.2
  179.1 27.6 reduce-scatter.1
where the time goes:
time: 218 us; the launch traced here: 215 us
  waiting for transfers between devices  110 us (50%)
  blocking collectives  58.2 us (27%)
  matrix products  21.1 us (10%)
  between operations  14.9 us (7%)
  local copies, waits for them, and re-layouts  7.23 us (3%)
  other arithmetic  3.57 us (2%)
    unnamed x3, waiting for transfers between devices  82.1 us
    reduce_scatter x1, waiting for transfers between devices, body(): moe = lax.psum_scatter(weighted, 'grp', scatter_dimension=1, tiled=True)  27.8 us
    all_to_all x1, blocking collectives, body(): lax.all_to_all(produced, 'head', split_axis=0, concat_axis=0, tiled=True)  15.1 us
    all_gather x1, blocking collectives, body(): lax.all_gather(residual, 'grp', axis=1, tiled=True).astype(jnp.float32)  14.9 us
    all_gather x1, blocking collectives, body(): lax.all_gather(attended, 'grp', axis=0, tiled=True)  14.4 us
    all_to_all x1, blocking collectives, body(): lax.all_to_all(outgoing, 'head', split_axis=0, concat_axis=0, tiled=True)  13.8 us
    dot_general x1, matrix products, expert_rows(): lax.dot_general(flattened, up_local, contract, preferred_element_type=jnp...  5.17 us
    dot_general x1, matrix products, expert_rows(): lax.dot_general(flattened, gate_local, contract, preferred_element_type=j...  5.12 us
  transfers between devices with their start and end apart: 2, of which 2 were waited for; matrix products, arithmetic and copies ran while one was open for 1% of the time, Pallas kernels for 0%

commit v1 on v0

--- a/solution.py
+++ b/solution.py
@@ -9,15 +9,12 @@
 EPSILON = 1e-06
 
 
-def expert_rows(slot_rows, gate_local, up_local, down_local):
-    sources, slots, width = slot_rows.shape
-    flattened = slot_rows.reshape(sources * slots, width)
+def expert_rows(flattened, gate_local, up_local, down_local):
     contract = (((1,), (1,)), ((), ()))
     gate_out = lax.dot_general(flattened, gate_local, contract, preferred_element_type=jnp.float32)
     upward = lax.dot_general(flattened, up_local, contract, preferred_element_type=jnp.float32)
     activated = (jax.nn.silu(gate_out) * upward).astype(jnp.bfloat16)
-    produced = jnp.dot(activated, down_local, preferred_element_type=jnp.float32)
-    return produced.reshape(sources, slots, down_local.shape[1])
+    return jnp.dot(activated, down_local, preferred_element_type=jnp.float32)
 
 
 def body(
@@ -65,12 +62,25 @@
         * attn_gain.reshape(head_count, head_size)
     )
     attended = scaled.astype(jnp.bfloat16).reshape(requests_here * positions, width_here)
-    partial_sums = jnp.dot(
-        lax.all_gather(attended, "grp", axis=0, tiled=True),
-        out_proj,
-        preferred_element_type=jnp.float32,
+    groups = lax.axis_size("grp")
+    heads = lax.axis_size("head")
+    rows_here = requests_here * positions
+    everyone = lax.all_to_all(
+        jnp.broadcast_to(attended[None], (groups, rows_here, width_here)),
+        "grp",
+        split_axis=0,
+        concat_axis=0,
+        tiled=True,
+    ).reshape(groups * rows_here, width_here)
+    partial_sums = jnp.dot(everyone, out_proj, preferred_element_type=jnp.float32)
+    shares = lax.all_to_all(
+        partial_sums.astype(jnp.bfloat16).reshape(heads, -1, partial_sums.shape[1]),
+        "head",
+        split_axis=0,
+        concat_axis=0,
+        tiled=True,
     )
-    mixed = lax.psum_scatter(partial_sums, "head", scatter_dimension=0, tiled=True)
+    mixed = jnp.sum(shares.astype(jnp.float32), axis=0)
     tokens_here = mixed.shape[0]
     columns = mixed.shape[1]
     model_width = columns * lax.axis_size("grp")
@@ -97,31 +107,45 @@
     gate_local = expert_gate[0]
     up_local = expert_up[0]
     down_local = expert_down[0]
-    full_rows = lax.all_gather(residual, "grp", axis=1, tiled=True).astype(jnp.float32)
+    slot_rows = (
+        jnp.dot(picker, residual, preferred_element_type=jnp.float32)
+        .astype(jnp.bfloat16)
+        .reshape(1, experts, CAP, columns)
+    )
+    arrived = lax.all_to_all(
+        jnp.broadcast_to(slot_rows, (groups, experts, CAP, columns)).reshape(-1, CAP, columns),
+        ("grp", "head"),
+        split_axis=0,
+        concat_axis=0,
+        tiled=True,
+    )
+    full_rows = (
+        arrived.reshape(groups, heads * CAP, columns)
+        .transpose(1, 0, 2)
+        .reshape(heads * CAP, model_width)
+        .astype(jnp.float32)
+    )
     normed = (
         full_rows
         * lax.rsqrt(jnp.mean(full_rows * full_rows, axis=-1, keepdims=True) + EPSILON)
         * ffn_gain
     ).astype(jnp.bfloat16)
+    produced = expert_rows(normed, gate_local, up_local, down_local)
     outgoing = (
-        jnp.dot(picker, normed, preferred_element_type=jnp.float32)
-        .astype(jnp.bfloat16)
-        .reshape(experts, CAP, model_width)
+        produced.astype(jnp.bfloat16)
+        .reshape(heads * CAP, groups, columns)
+        .transpose(1, 0, 2)
+        .reshape(-1, CAP, columns)
     )
-    produced = expert_rows(
-        lax.all_to_all(outgoing, "head", split_axis=0, concat_axis=0, tiled=True),
-        gate_local,
-        up_local,
-        down_local,
-    )
-    returned = lax.all_to_all(produced, "head", split_axis=0, concat_axis=0, tiled=True)
-    weighted = jnp.dot(
+    returned = lax.all_to_all(
+        outgoing, ("grp", "head"), split_axis=0, concat_axis=0, tiled=True
+    ).reshape(groups, slots_all, columns)
+    moe = jnp.dot(
         combiner,
-        returned.reshape(slots_all, model_width),
+        jnp.sum(returned.astype(jnp.float32), axis=0),
         precision=lax.Precision.HIGHEST,
         preferred_element_type=jnp.float32,
     )
-    moe = lax.psum_scatter(weighted, "grp", scatter_dimension=1, tiled=True)
     stream_out = (residual.astype(jnp.float32) + moe).astype(jnp.bfloat16).reshape(stream_in.shape)
     return (stream_out, memory_state)
 

time: 218 us -> 89.8 us (0.41); the launches traced: 215 us -> 89.2 us
  waiting for transfers between devices: 110 us -> 23.7 us
  blocking collectives: 58.2 us -> 16.5 us
  starting transfers between devices: 0.08 us -> 19.5 us
  between operations: 14.9 us -> 0.89 us
    unnamed x3 -> x0, waiting for transfers between devices: 82.1 us -> none
    all_gather x2 -> x0, blocking collectives: 29.3 us -> none  [the longest x1 14.9 us: body(): lax.all_gather(residual, 'grp', axis=1, tiled=True).astype(jnp.float32)]
    reduce_scatter x1 -> x0, waiting for transfers between devices: 27.8 us -> none  [body(): moe = lax.psum_scatter(weighted, 'grp', scatter_dimension=1, tiled=True)]
    all_to_all x0 -> x3, waiting for transfers between devices: none -> 23.7 us  [the longest x1 12.5 us: body(): lax.all_to_all(jnp.broadcast_to(slot_rows, (groups, experts, CAP, columns...]
    all_to_all x0 -> x3, starting transfers between devices: none -> 19.5 us  [the longest x1 7.77 us: body(): lax.all_to_all(partial_sums.astype(jnp.bfloat16).reshape(heads, -1, parti...]
    all_to_all x2 -> x1, blocking collectives: 28.9 us -> 16.5 us  [body(): lax.all_to_all(outgoing, ('grp', 'head'), split_axis=0, concat_axis=0, ti...]
    dot_general x5 -> x4, matrix products: 12 us -> 9.95 us  [the longest x1 8.64 us: expert_rows(): return jnp.dot(activated, down_local, preferred_element_type=jnp.float32)]
  transfers between devices with their start and end apart: 2 -> 3, of which waited for: 2 -> 3; matrix products, arithmetic and copies ran while one was open for 1% -> 1% of each run, Pallas kernels for 0% -> 0%
where the time goes in v1:
time: 89.8 us; the launch traced here: 89.2 us
  waiting for transfers between devices  23.7 us (26%)
  starting transfers between devices  19.5 us (22%)
  matrix products  19 us (21%)
  blocking collectives  16.5 us (18%)
  local copies, waits for them, and re-layouts  7.09 us (8%)
  other arithmetic  2.33 us (3%)
    all_to_all x1, blocking collectives, body(): lax.all_to_all(outgoing, ('grp', 'head'), split_axis=0, concat_axis=0, ti...  16.5 us
    all_to_all x1, waiting for transfers between devices, body(): lax.all_to_all(jnp.broadcast_to(slot_rows, (groups, experts, CAP, columns...  12.5 us
    dot_general x1, matrix products, expert_rows(): return jnp.dot(activated, down_local, preferred_element_type=jnp.float32)  8.64 us
    all_to_all x1, starting transfers between devices, body(): lax.all_to_all(partial_sums.astype(jnp.bfloat16).reshape(heads, -1, parti...  7.77 us
    all_to_all x1, waiting for transfers between devices, body(): lax.all_to_all(partial_sums.astype(jnp.bfloat16).reshape(heads, -1, parti...  6.61 us
    all_to_all x1, starting transfers between devices, body(): lax.all_to_all(jnp.broadcast_to(slot_rows, (groups, experts, CAP, columns...  5.96 us
    all_to_all x1, starting transfers between devices, body(): lax.all_to_all(jnp.broadcast_to(attended[None], (groups, rows_here, width...  5.8 us
    dot_general x1, matrix products, expert_rows(): lax.dot_general(flattened, gate_local, contract, preferred_element_type=j...  5.12 us
  transfers between devices with their start and end apart: 3, of which 3 were waited for; matrix products, arithmetic and copies ran while one was open for 1% of the time, Pallas kernels for 0%

profile of v1, /device:TPU:1, one launch (start us, length us, event | category | flops | bytes accessed | tf_op | source)
XLA Modules:
  0.0 89.2 jit_solution(7887392764341729980)
XLA Ops:
  0.6 0.0 copy-start
  0.6 0.0 copy-start.1
  0.7 0.0 copy-start.6
  0.7 0.9 reshape.153
  1.6 0.7 reshape.149
  2.3 0.7 reshape.151
  3.1 2.9 %fusion.9 = f32[8,4,1,128]{3,2,1,0:T(1,128)S(1)} fusion(f32[8,4,128,128]{3,2,1,0:T(8,128)} %param.18, f32[8,4,128]{2,1,0:T(4,128)S(1)} %get-tuple-element.8, f32[8,4,128]{2,1,0:T(4,128)S(1)} %get-tuple-element.11, f32[4]{0:T(128)} %param.17, bf16[8,4,128,1]{2,1,0,3:T(4,128)(2,1)S(1)} %get-tuple-element.4), kind=kOutput, calls=%fused_computation.9 | convolution fusion | flops 7864320 | bytes 2154512 | tf_op jit(solution)/shard_map/rhk,rhkv->rhv/dot_general | solution.py:54
  6.0 0.0 copy-done.1
  6.0 0.0 copy-done.6
  6.0 1.3 %multiply_add_fusion = f32[8,4,128,128]{3,2,1,0:T(8,128)S(1)} fusion(f32[8,4,128,128]{3,2,1,0:T(8,128)S(1)} %copy-done.1, f32[8,4,128]{2,1,0:T(4,128)S(1)} %get-tuple-element.9, f32[8,4,128]{2,1,0:T(4,128)S(1)} %get-tuple-element.10, f32[8,4,128]{2,1,0:T(4,128)S(1)} %get-tuple-element.8, f32[8,4,128]{2,1,0:T(4,128)S(1)} %get-tuple-element.11, f32[4]{0:T(128)S(1)} %copy-done.6), kind=kLoop, calls=%fused_computation.7 | loop fusion | flops 3145728 | bytes 4259856 | tf_op jit(solution)/shard_map/add | solution.py:52
  7.3 0.0 copy-start.2
  7.3 0.0 copy-start.7
  7.3 0.0 copy-start.5
  7.3 0.0 copy-start.8
  7.4 1.3 %copy-done.2 = f32[8,4,128,128]{3,2,1,0:T(8,128)} copy-done((f32[8,4,128,128]{3,2,1,0:T(8,128)}, f32[8,4,128,128]{3,2,1,0:T(8,128)S(1)}, u32[]{:S(2)}) %copy-start.2) | copy-done | bytes 2097176
  8.6 0.0 copy-start.4
  8.6 1.1 %fusion.32 = f32[8,4,1,128]{3,2,1,0:T(1,128)S(1)} fusion(f32[8,4,128,128]{3,2,1,0:T(8,128)S(1)} %multiply_add_fusion, bf16[8,4,128,1]{2,1,0,3:T(4,128)(2,1)S(1)} %get-tuple-element.5), kind=kOutput, calls=%fused_computation.37 | convolution fusion | flops 6291456 | bytes 2121728 | tf_op jit(solution)/shard_map/rhk,rhkv->rhv/dot_general | solution.py:54
  9.7 0.0 copy-start.3
  9.7 0.1 multiply_reduce_fusion.1
  9.8 0.1 fusion.31
  9.9 0.0 copy-done.7
  9.9 0.6 broadcast_in_dim.6
  10.6 5.8 %all-to-all-start = ((bf16[8,16,512]{2,1,0:T(8,128)(2,1)}), bf16[8,16,512]{2,1,0:T(8,128)(2,1)S(1)}, u32[]{:S(2)}, u32[]{:S(2)}) async-start(bf16[8,16,512]{2,1,0:T(8,128)(2,1)} %broadcast_in_dim.6), calls=%async_computation | async-start | bytes 262144 | tf_op jit(solution)/shard_map/all_to_all | solution.py:68
  16.4 0.0 copy-done.5
  16.4 0.1 copy.54
  16.5 0.1 copy.53
  16.6 0.1 mul.113
  16.7 0.0 copy-done.8
  16.7 0.1 copy.56
  16.8 0.1 mul.115
  16.9 0.1 eq.30
  17.0 0.1 fusion.39
  17.1 4.6 %all-to-all-done = bf16[8,16,512]{2,1,0:T(8,128)(2,1)S(1)} async-done(((bf16[8,16,512]{2,1,0:T(8,128)(2,1)}), bf16[8,16,512]{2,1,0:T(8,128)(2,1)S(1)}, u32[]{:S(2)}, u32[]{:S(2)}) %all-to-all-start) | async-done | bytes 131104 | tf_op jit(solution)/shard_map/all_to_all | solution.py:68
  21.7 0.0 copy-done
  21.7 0.9 %fusion.10 = bf16[16,8,768]{2,1,0:T(8,128)(2,1)} fusion(bf16[128,512]{1,0:T(8,128)(2,1)S(1)} %bitcast.95, bf16[512,768]{1,0:T(8,128)(2,1)S(1)} %copy-done), kind=kOutput, calls=%fused_computation.11 | convolution fusion | flops 100761600 | bytes 1114112 | tf_op jit(solution)/shard_map/dot_general | solution.py:75
  22.6 7.8 %all-to-all-start.1 = ((bf16[16,8,768]{2,1,0:T(8,128)(2,1)}), bf16[16,8,768]{2,1,0:T(8,128)(2,1)S(1)}, u32[]{:S(2)}, u32[]{:S(2)}) async-start(bf16[16,8,768]{2,1,0:T(8,128)(2,1)} %fusion.10), calls=%async_computation.1 | async-start | bytes 393216 | tf_op jit(solution)/shard_map/all_to_all | solution.py:76
  30.4 0.2 select_reduce_fusion.1
  30.6 0.1 reshape.158
  30.7 0.1 copy.55
  30.7 0.0 copy-done.4
  30.8 0.1 convert_reduce_fusion.1
  30.8 6.6 %all-to-all-done.1 = bf16[16,8,768]{2,1,0:T(8,128)(2,1)S(1)} async-done(((bf16[16,8,768]{2,1,0:T(8,128)(2,1)}), bf16[16,8,768]{2,1,0:T(8,128)(2,1)S(1)}, u32[]{:S(2)}, u32[]{:S(2)}) %all-to-all-start.1) | async-done | bytes 196640 | tf_op jit(solution)/shard_map/all_to_all | solution.py:76
  37.5 0.2 convolution_convert_fusion.1
  37.7 0.9 %broadcast_in_dim.8 = bf16[8,16,2,768]{3,2,1,0:T(2,128)(2,1)} broadcast(bf16[16,2,768]{2,1,0:T(2,128)(2,1)S(1)} %broadcast_in_dim.7), dimensions={1,2,3} | broadcast | bytes 442368 | tf_op jit(solution)/shard_map/broadcast_in_dim | solution.py:116
  38.7 6.0 %all-to-all-start.2 = ((bf16[128,2,768]{2,1,0:T(2,128)(2,1)}), bf16[128,2,768]{2,1,0:T(2,128)(2,1)S(1)}, u32[]{:S(2)}, u32[]{:S(2)}) async-start(bf16[128,2,768]{2,1,0:T(2,128)(2,1)} %bitcast.16), calls=%async_computation.2 | async-start | bytes 786432 | tf_op jit(solution)/shard_map/all_to_all | solution.py:115
  44.6 0.0 copy-done.3
  44.7 12.5 %all-to-all-done.2 = bf16[128,2,768]{2,1,0:T(2,128)(2,1)S(1)} async-done(((bf16[128,2,768]{2,1,0:T(2,128)(2,1)}), bf16[128,2,768]{2,1,0:T(2,128)(2,1)S(1)}, u32[]{:S(2)}, u32[]{:S(2)}) %all-to-all-start.2) | async-done | bytes 393248 | tf_op jit(solution)/shard_map/all_to_all | solution.py:115
  57.2 0.1 reshape.169
  57.3 0.2 multiply_reduce_fusion
  57.5 0.1 fusion.23
  57.7 5.1 %fusion.4 = f32[32,576]{1,0:T(8,128)S(1)} fusion(bf16[32,6144]{1,0:T(8,128)(2,1)S(1)} %bitcast.91, bf16[1,576,6144]{2,1,0:T(8,128)(2,1)} %param.23), kind=kOutput, calls=%fused_computation.4 | convolution fusion | flops 226492416 | bytes 7544832 | tf_op jit(solution)/shard_map/dot_general | solution.py:14
  62.8 8.6 %fusion.6 = bf16[32,6144]{1,0:T(8,128)(2,1)S(1)} fusion(bf16[1,576,6144]{2,1,0:T(8,128)(2,1)} %param.25, bf16[32,6144]{1,0:T(8,128)(2,1)S(1)} %bitcast.92, bf16[1,576,6144]{2,1,0:T(8,128)(2,1)} %param.24, f32[32,576]{1,0:T(8,128)S(1)} %fusion.4), kind=kOutput, calls=%fused_computation.6 | convolution fusion | flops 453292032 | bytes 15015936 | tf_op jit(solution)/shard_map/dot_general | solution.py:17
  71.5 0.1 reshape.161
  71.7 16.5 %all_to_all.20 = bf16[128,2,768]{2,1,0:T(2,128)(2,1)S(1)} all-to-all(bf16[128,2,768]{2,1,0:T(2,128)(2,1)S(1)} %reshape.161), channel_id=1, replica_groups=mesh['grp'=8,'head'=16] {'grp','head'}, dimensions={0} | all-to-all | bytes 786432 | tf_op jit(solution)/shard_map/all_to_all | solution.py:140
  88.2 0.1 reshape.170
  88.4 0.2 fusion.17
  88.6 0.6 reshape.162
  (16 shorter events, 0.3 us)
Async XLA Ops:
  0.6 21.0 %copy-start = (bf16[512,768]{1,0:T(8,128)(2,1)S(1)}, bf16[512,768]{1,0:T(8,128)(2,1)}, u32[]{:S(2)}) copy-start(bf16[512,768]{1,0:T(8,128)(2,1)} %param.20) | copy-start | bytes 2359300
  0.6 5.3 %copy-start.1 = (f32[8,4,128,128]{3,2,1,0:T(8,128)S(1)}, f32[8,4,128,128]{3,2,1,0:T(8,128)}, u32[]{:S(2)}) copy-start(f32[8,4,128,128]{3,2,1,0:T(8,128)} %param.18) | copy-start | bytes 6291460
  0.7 5.3 %copy-start.6 = (f32[4]{0:T(128)S(1)}, f32[4]{0:T(128)}, u32[]{:S(2)}) copy-start(f32[4]{0:T(128)} %param.17) | copy-start | bytes 52
  7.3 1.3 %copy-start.2 = (f32[8,4,128,128]{3,2,1,0:T(8,128)}, f32[8,4,128,128]{3,2,1,0:T(8,128)S(1)}, u32[]{:S(2)}) copy-start(f32[8,4,128,128]{3,2,1,0:T(8,128)S(1)} %multiply_add_fusion) | copy-start | bytes 6291460
  7.3 2.6 %copy-start.7 = (f32[512]{0:T(512)S(1)}, f32[512]{0:T(512)}, u32[]{:S(2)}) copy-start(f32[512]{0:T(512)} %param.19) | copy-start | bytes 6148
  7.3 9.1 %copy-start.5 = (s32[4,2,2]{0,2,1:T(2,128)S(1)}, s32[4,2,2]{0,2,1:T(2,128)}, u32[]{:S(2)}) copy-start(s32[4,2,2]{0,2,1:T(2,128)} %param.26) | copy-start | bytes 196
  7.3 9.3 %copy-start.8 = (f32[4,2,2]{0,2,1:T(2,128)S(1)}, f32[4,2,2]{0,2,1:T(2,128)}, u32[]{:S(2)}) copy-start(f32[4,2,2]{0,2,1:T(2,128)} %param.27) | copy-start | bytes 196
  8.6 22.1 %copy-start.4 = (bf16[4,2,768]{2,1,0:T(2,128)(2,1)S(1)}, bf16[4,2,768]{2,1,0:T(2,128)(2,1)}, u32[]{:S(2)}) copy-start(bf16[4,2,768]{2,1,0:T(2,128)(2,1)} %param.21) | copy-start | bytes 36868
  9.7 35.0 %copy-start.3 = (f32[6144]{0:T(1024)S(1)}, f32[6144]{0:T(1024)}, u32[]{:S(2)}) copy-start(f32[6144]{0:T(1024)} %param.22) | copy-start | bytes 73732
  10.6 11.1 %all-to-all-start = ((bf16[8,16,512]{2,1,0:T(8,128)(2,1)}), bf16[8,16,512]{2,1,0:T(8,128)(2,1)S(1)}, u32[]{:S(2)}, u32[]{:S(2)}) async-start(bf16[8,16,512]{2,1,0:T(8,128)(2,1)} %broadcast_in_dim.6), calls=%async_computation | async-start | bytes 262144 | tf_op jit(solution)/shard_map/all_to_all | solution.py:68
  22.6 14.8 %all-to-all-start.1 = ((bf16[16,8,768]{2,1,0:T(8,128)(2,1)}), bf16[16,8,768]{2,1,0:T(8,128)(2,1)S(1)}, u32[]{:S(2)}, u32[]{:S(2)}) async-start(bf16[16,8,768]{2,1,0:T(8,128)(2,1)} %fusion.10), calls=%async_computation.1 | async-start | bytes 393216 | tf_op jit(solution)/shard_map/all_to_all | solution.py:76
  38.7 18.5 %all-to-all-start.2 = ((bf16[128,2,768]{2,1,0:T(2,128)(2,1)}), bf16[128,2,768]{2,1,0:T(2,128)(2,1)S(1)}, u32[]{:S(2)}, u32[]{:S(2)}) async-start(bf16[128,2,768]{2,1,0:T(2,128)(2,1)} %bitcast.16), calls=%async_computation.2 | async-start | bytes 786432 | tf_op jit(solution)/shard_map/all_to_all | solution.py:115

commit v2 on v1

v2 whole, which is shorter than its diff:
```python
import jax
import jax.numpy as jnp
from jax import lax
from jax.experimental import pallas as pl
from jax.experimental.pallas import tpu as pltpu
from jax.sharding import PartitionSpec as P

CAP = 2
HIDDEN_STEPS = 4
DOWN_STEPS = 4
AHEAD = 4


EPSILON = 1e-06


def in_hbm(array):
    return pltpu.with_memory_space_constraint(array, pltpu.HBM)


ROWS_CONTRACT = (((1,), (1,)), ((), ()))


def readout_kernel(
    query_in, key_in, value_in, decay_in, gain_in, states_ref, out_ref,
    query_ref, key_ref, value_ref, decay_ref, gain_ref, held, read, rows, small_sems, sems,
):
    requests, positions, _ = query_ref.shape
    heads, size = states_ref.shape[1], states_ref.shape[2]
    small = [
        pltpu.make_async_copy(source, target, small_sems.at[index])
        for index, (source, target) in enumerate(
            (
                (query_in, query_ref),
                (key_in, key_ref),
                (value_in, value_ref),
                (decay_in, decay_ref),
                (gain_in, gain_ref),
            )
        )
    ]
    small[0].start()
    copies = [
        pltpu.make_async_copy(states_ref.at[request], held.at[request], sems.at[request])
        for request in range(requests)
    ]
    for copy in copies:
        copy.start()
    for copy in small[1:]:
        copy.start()
    small[0].wait()
    for request in range(requests):
        copies[request].wait()
        for head in range(heads):
            columns = slice(head * size, (head + 1) * size)
            state = held[request, head]
            high = state.astype(jnp.bfloat16)
            low = (state - high.astype(jnp.float32)).astype(jnp.bfloat16)
            query = query_ref[request, :, columns]
            read[request, :, columns] = jnp.dot(
                jnp.concatenate([query, query], axis=1),
                jnp.concatenate([high, low], axis=0),
                preferred_element_type=jnp.float32,
            )
    for copy in small[1:]:
        copy.wait()
    first = lax.broadcasted_iota(jnp.int32, (requests, positions, size), 1) == 0
    for head in range(heads):
        columns = slice(head * size, (head + 1) * size)
        decay = decay_ref[head]
        query = query_ref[:, :, columns].astype(jnp.float32)
        keys = key_ref[:, :, columns].astype(jnp.float32)
        values = value_ref[:, :, columns].astype(jnp.float32)
        with_first = jnp.sum(query * keys[:, 0:1, :], axis=2, keepdims=True) * values[:, 0:1, :]
        with_own = jnp.sum(query * keys, axis=2, keepdims=True) * values
        once = decay * read[:, :, columns] + with_first
        readout = jnp.where(first, once, decay * once + with_own)
        scaled = (
            readout
            * lax.rsqrt(jnp.mean(readout * readout, axis=2, keepdims=True) + EPSILON)
            * gain_ref[0:1, columns][None]
        )
        for request in range(requests):
            rows[request * positions : (request + 1) * positions, columns] = scaled[request]
    attended = rows[...].astype(jnp.bfloat16)
    for copy in range(out_ref.shape[0]):
        out_ref[copy] = attended


def readouts(query_in, key_in, value_in, decay_rate, attn_gain, states, copies):
    requests, positions, width = query_in.shape
    vmem = pl.BlockSpec(memory_space=pltpu.VMEM)
    return pl.pallas_call(
        readout_kernel,
        out_shape=jax.ShapeDtypeStruct((copies, requests * positions, width), jnp.bfloat16),
        in_specs=[pl.BlockSpec(memory_space=pltpu.HBM)] * 6,
        out_specs=vmem,
        scratch_shapes=[
            pltpu.VMEM(query_in.shape, jnp.bfloat16),
            pltpu.VMEM(query_in.shape, jnp.bfloat16),
            pltpu.VMEM(query_in.shape, jnp.bfloat16),
            pltpu.SMEM(decay_rate.shape, jnp.float32),
            pltpu.VMEM((1, width), jnp.float32),
            pltpu.VMEM(states.shape, jnp.float32),
            pltpu.VMEM(query_in.shape, jnp.float32),
            pltpu.VMEM((requests * positions, width), jnp.float32),
            pltpu.SemaphoreType.DMA((5,)),
            pltpu.SemaphoreType.DMA((requests,)),
        ],
        compiler_params=pltpu.CompilerParams(vmem_limit_bytes=32 * 2**20),
        cost_estimate=pl.CostEstimate(flops=10**7, bytes_accessed=states.size * 4, transcendentals=0),
        name="readouts",
    )(*(in_hbm(array) for array in (query_in, key_in, value_in, decay_rate, attn_gain.reshape(1, width), states)))


def experts_kernel(
    rows_ref, gain_ref, gate_in, up_in, down_in, out_ref, normed, gate_ref, up_ref, down_ref, activated, sems
):
    hidden, width = gate_in.shape
    columns = rows_ref.shape[2]
    shards = width // columns
    rows = rows_ref.shape[0] * rows_ref.shape[1] // shards
    blocks = rows_ref.shape[0] // shards
    tile = hidden // HIDDEN_STEPS
    wide = shards // DOWN_STEPS
    steps = HIDDEN_STEPS + DOWN_STEPS

    def copies(step):
        if step < HIDDEN_STEPS:
            cut = pl.ds(step * tile, tile)
            parts = ((gate_in.at[cut], gate_ref.at[cut]), (up_in.at[cut], up_ref.at[cut]))
        else:
            cut = pl.ds((step - HIDDEN_STEPS) * wide * columns, wide * columns)
            halves = (pl.ds(0, hidden // 2), pl.ds(hidden // 2, hidden // 2))
            parts = [(down_in.at[half, cut], down_ref.at[half, cut]) for half in halves]
        return [
            pltpu.make_async_copy(source, target, sems.at[step, index])
            for index, (source, target) in enumerate(parts)
        ]

    def begin(step):
        if step < steps:
            for copy in copies(step):
                copy.start()

    def finish(step):
        for copy in copies(step):
            copy.wait()
        begin(step + AHEAD)

    for step in range(AHEAD):
        begin(step)
    squares = jnp.zeros((rows, 1), jnp.float32)
    for shard in range(shards):
        arrived = rows_ref[shard * blocks : (shard + 1) * blocks].reshape(rows, columns)
        normed[:, shard * columns : (shard + 1) * columns] = arrived
        arrived = arrived.astype(jnp.float32)
        squares = squares + jnp.sum(arrived * arrived, axis=1, keepdims=True)
    scale = lax.rsqrt(squares / width + EPSILON)
    for shard in range(shards):
        cut = slice(shard * columns, (shard + 1) * columns)
        normed[:, cut] = (normed[:, cut].astype(jnp.float32) * scale * gain_ref[:, cut]).astype(jnp.bfloat16)
    for step in range(HIDDEN_STEPS):
        finish(step)
        cut = slice(step * tile, (step + 1) * tile)
        gate = lax.dot_general(gate_ref[cut], normed[...], ROWS_CONTRACT, preferred_element_type=jnp.float32)
        upward = lax.dot_general(up_ref[cut], normed[...], ROWS_CONTRACT, preferred_element_type=jnp.float32)
        activated[cut, :] = (gate / (1.0 + jnp.exp(-gate)) * upward).astype(jnp.bfloat16)
    for step in range(DOWN_STEPS):
        finish(HIDDEN_STEPS + step)
        for shard in range(step * wide, (step + 1) * wide):
            produced = lax.dot_general(
                activated[...],
                down_ref[:, shard * columns : (shard + 1) * columns],
                (((0,), (0,)), ((), ())),
                preferred_element_type=jnp.float32,
            )
            out_ref[shard * blocks : (shard + 1) * blocks] = produced.astype(jnp.bfloat16).reshape(
                blocks, rows // blocks, columns
            )


def expert_rows(arrived, gain, gate, up, down):
    hidden, width = gate.shape
    rows = arrived.shape[0] * arrived.shape[1] * arrived.shape[2] // width
    vmem = pl.BlockSpec(memory_space=pltpu.VMEM)
    hbm = pl.BlockSpec(memory_space=pl.ANY)
    return pl.pallas_call(
        experts_kernel,
        out_shape=jax.ShapeDtypeStruct(arrived.shape, jnp.bfloat16),
        in_specs=[vmem, vmem, hbm, hbm, hbm],
        out_specs=vmem,
        scratch_shapes=[
            pltpu.VMEM((rows, width), jnp.bfloat16),
            pltpu.VMEM((hidden, width), jnp.bfloat16),
            pltpu.VMEM((hidden, width), jnp.bfloat16),
            pltpu.VMEM((hidden, width), jnp.bfloat16),
            pltpu.VMEM((hidden, rows), jnp.bfloat16),
            pltpu.SemaphoreType.DMA((HIDDEN_STEPS + DOWN_STEPS, 2)),
        ],
        compiler_params=pltpu.CompilerParams(vmem_limit_bytes=48 * 2**20),
        cost_estimate=pl.CostEstimate(flops=6 * rows * hidden * width, bytes_accessed=6 * hidden * width, transcendentals=0),
        name="experts",
    )(arrived, gain.reshape(1, width), in_hbm(gate), in_hbm(up), in_hbm(down))


def body(
    query_in,
    key_in,
    value_in,
    decay_rate,
    states,
    attn_gain,
    out_proj,
    stream_in,
    ffn_gain,
    expert_gate,
    expert_up,
    expert_down,
    routes,
    route_weights,
):
    requests_here, positions, width_here = query_in.shape
    head_count = states.shape[1]
    head_size = states.shape[2]
    shape_four = (requests_here, positions, head_count, head_size)
    groups = lax.axis_size("grp")
    heads = lax.axis_size("head")
    rows_here = requests_here * positions
    attended = readouts(query_in, key_in, value_in, decay_rate, attn_gain, states, groups)
    attended, keys, values, decay, chosen, weighting, stream = lax.optimization_barrier(
        (attended, key_in, value_in, decay_rate, routes, route_weights, stream_in)
    )
    everyone = lax.all_to_all(attended, "grp", split_axis=0, concat_axis=0, tiled=True)
    keyset = keys.astype(jnp.float32).reshape(shape_four)
    valueset = values.astype(jnp.float32).reshape(shape_four)
    memory_state = states
    for position in range(positions):
        memory_state = (
            decay[None, :, None, None] * memory_state
            + keyset[:, position, :, :, None] * valueset[:, position, :, None, :]
        )
    tokens_here = stream_in.shape[0] * positions
    columns = stream_in.shape[2]
    stream = stream.astype(jnp.float32).reshape(tokens_here, columns)
    experts = lax.axis_size("head") * expert_gate.shape[0]
    chosen = chosen.reshape(tokens_here, 2)
    weighting = weighting.reshape(tokens_here, 2)
    onehot = (
        (chosen[:, :, None] == jnp.arange(experts, dtype=jnp.int32)[None, None, :])
        .astype(jnp.int32)
        .reshape(tokens_here * 2, experts)
    )
    earlier = jnp.cumsum(onehot, axis=0) - onehot
    slot_index = jnp.sum(earlier * onehot, axis=1).reshape(tokens_here, 2)
    slot_code = chosen * CAP + slot_index
    slots_all = experts * CAP
    selection = (
        jnp.arange(slots_all, dtype=jnp.int32)[:, None, None] == slot_code[None, :, :]
    ).astype(jnp.float32)
    picker = jnp.sum(selection, axis=2).astype(jnp.bfloat16)
    combiner = jnp.transpose(jnp.sum(selection * weighting[None, :, :], axis=2))
    everyone, memory_state, stream, picker, combiner = lax.optimization_barrier(
        (everyone, memory_state, stream, picker, combiner)
    )
    partial_sums = jnp.dot(
        everyone.reshape(groups * rows_here, width_here), out_proj, preferred_element_type=jnp.float32
    )
    shares = lax.all_to_all(
        partial_sums.astype(jnp.bfloat16).reshape(heads, -1, partial_sums.shape[1]),
        "head",
        split_axis=0,
        concat_axis=0,
        tiled=True,
    )
    mixed = jnp.sum(shares.astype(jnp.float32), axis=0)
    residual = (stream + mixed).astype(jnp.bfloat16)
    slot_rows = (
        jnp.dot(picker, residual, preferred_element_type=jnp.float32)
        .astype(jnp.bfloat16)
        .reshape(1, experts, CAP, columns)
    )
    arrived = lax.all_to_all(
        jnp.broadcast_to(slot_rows, (groups, experts, CAP, columns)).reshape(-1, CAP, columns),
        ("grp", "head"),
        split_axis=0,
        concat_axis=0,
        tiled=True,
    )
    outgoing = expert_rows(arrived, ffn_gain, expert_gate[0], expert_up[0], expert_down[0])
    returned = lax.all_to_all(
        outgoing, ("grp", "head"), split_axis=0, concat_axis=0, tiled=True
    ).reshape(groups, slots_all, columns)
    moe = jnp.dot(
        combiner,
        jnp.sum(returned.astype(jnp.float32), axis=0),
        precision=lax.Precision.HIGHEST,
        preferred_element_type=jnp.float32,
    )
    stream_out = (residual.astype(jnp.float32) + moe).astype(jnp.bfloat16).reshape(stream_in.shape)
    return (stream_out, memory_state)


def solution(mesh):
    return jax.shard_map(
        body,
        mesh=mesh,
        in_specs=(
            P("grp", None, "head"),
            P("grp", None, "head"),
            P("grp", None, "head"),
            P("head"),
            P("grp", "head", None, None),
            P("head"),
            P("head", "grp"),
            P("head", None, "grp"),
            P(),
            P("head", "grp", None),
            P("head", "grp", None),
            P("head", "grp", None),
            P("head", None, None),
            P("head", None, None),
        ),
        out_specs=(P("head", None, "grp"), P("grp", "head", None, None)),
        check_vma=False,
    )
```

time: 89.8 us -> 74.9 us (0.83)
  blocking collectives: 16.5 us -> 49.5 us
  waiting for transfers between devices: 23.7 us -> 1.75 us
  matrix products: 19 us -> 0.64 us
  starting transfers between devices: 19.5 us -> 5.81 us
  Pallas kernels: 0 us -> 11.6 us
  local copies, waits for them, and re-layouts: 7.09 us -> 1.77 us
    all_to_all x0 -> x2, blocking collectives: none -> 33 us  [the longest x1 18.3 us: body(): lax.all_to_all(jnp.broadcast_to(slot_rows, (groups, experts, CAP, columns...]
    all_to_all x3 -> x1, waiting for transfers between devices: 23.7 us -> 1.75 us  [body(): lax.all_to_all(attended, 'grp', split_axis=0, concat_axis=0, tiled=True)]
    dot_general x5 -> x1, matrix products: 18.7 us -> 0.28 us  [body(): jnp.dot(everyone.reshape(groups * rows_here, width_here), out_proj, prefe...]
    all_to_all x3 -> x1, starting transfers between devices: 19.5 us -> 5.81 us  [body(): lax.all_to_all(attended, 'grp', split_axis=0, concat_axis=0, tiled=True)]
    pallas_call x0 -> x2, Pallas kernels: none -> 11.6 us  [the longest x1 8.21 us: expert_rows(): pl.pallas_call(experts_kernel, out_shape=jax.ShapeDtypeStruct(arrived.sha...]
    reshape x6 -> x3, local copies, waits for them, and re-layouts: 2.56 us -> 0.05 us  [the longest x1 0.02 us: body(): keyset = keys.astype(jnp.float32).reshape(shape_four)]
    unnamed x20 -> x18, local copies, waits for them, and re-layouts: 1.52 us -> 0.04 us
    add x1, other arithmetic: 1.31 us -> 2.27 us  [body(): decay[None, :, None, None] * memory_state]
  transfers between devices with their start and end apart: 3 -> 1, of which waited for: 3 -> 1; matrix products, arithmetic and copies ran while one was open for 1% -> 5% of each run, Pallas kernels for 0% -> 0%
where the time goes in v2:
time: 74.9 us; the launch traced here: 74.6 us
  blocking collectives  49.5 us (66%)
  Pallas kernels  11.6 us (15%)
  starting transfers between devices  5.81 us (8%)
  other arithmetic  2.74 us (4%)
  local copies, waits for them, and re-layouts  1.77 us (2%)
  waiting for transfers between devices  1.75 us (2%)
  between operations  0.86 us (1%)
    all_to_all x1, blocking collectives, body(): lax.all_to_all(jnp.broadcast_to(slot_rows, (groups, experts, CAP, columns...  18.3 us
    all_to_all x1, blocking collectives, body(): lax.all_to_all(outgoing, ('grp', 'head'), split_axis=0, concat_axis=0, ti...  16.6 us
    all_to_all x1, blocking collectives, body(): lax.all_to_all(partial_sums.astype(jnp.bfloat16).reshape(heads, -1, parti...  14.6 us
    pallas_call x1, Pallas kernels, expert_rows(): pl.pallas_call(experts_kernel, out_shape=jax.ShapeDtypeStruct(arrived.sha...  8.21 us
    all_to_all x1, starting transfers between devices, body(): lax.all_to_all(attended, 'grp', split_axis=0, concat_axis=0, tiled=True)  5.81 us
    pallas_call x1, Pallas kernels, readouts(): pl.pallas_call(readout_kernel, out_shape=jax.ShapeDtypeStruct((copies, re...  3.36 us
    add x1, other arithmetic, body(): decay[None, :, None, None] * memory_state  2.27 us
    all_to_all x1, waiting for transfers between devices, body(): lax.all_to_all(attended, 'grp', split_axis=0, concat_axis=0, tiled=True)  1.75 us
  transfers between devices with their start and end apart: 1, of which 1 were waited for; matrix products, arithmetic and copies ran while one was open for 5% of the time, Pallas kernels for 0%

profile of v2, /device:TPU:1, one launch (start us, length us, event | category | flops | bytes accessed | tf_op | source)
XLA Modules:
  0.0 74.6 jit_solution(8401284956034091747)
XLA Ops:
  0.6 0.0 copy-start
  0.6 0.0 copy-start.2
  0.7 0.0 copy-start.7
  0.7 0.0 copy-start.4
  0.7 0.0 copy-start.3
  0.7 0.0 copy-start.8
  0.7 0.0 copy-start.6
  0.7 0.0 copy-start.5
  0.7 3.4 %readouts.1 = bf16[8,16,512]{2,1,0:T(8,128)(2,1)} custom-call(bf16[8,2,512]{2,1,0:T(2,128)(2,1)} %query_in.1, bf16[8,2,512]{2,1,0:T(2,128)(2,1)} %key_in.1, bf16[8,2,512]{2,1,0:T(2,128)(2,1)} %value_in.1, f32[4]{0:T(128)} %decay_in.1, f32[1,512]{1,0:T(1,128)} %bitcast.43, f32[8,4,128,128]{3,2,1,0:T(8,128)} %states_ref.1), custom_call_target="tpu_custom_call" | custom-call | flops 10000000 | bytes 2097152 | tf_op jit(solution)/shard_map/readouts/pallas_call | solution.py:93
  4.1 5.8 %all-to-all-start = ((bf16[8,16,512]{2,1,0:T(8,128)(2,1)}), bf16[8,16,512]{2,1,0:T(8,128)(2,1)S(1)}, u32[]{:S(2)}, u32[]{:S(2)}) async-start(bf16[8,16,512]{2,1,0:T(8,128)(2,1)} %readouts.1), calls=%async_computation | async-start | bytes 262144 | tf_op jit(solution)/shard_map/all_to_all | solution.py:234
  9.9 0.0 copy-done.6
  9.9 0.1 copy.41
  10.0 0.1 copy.40
  10.1 0.1 mul.85
  10.2 0.0 copy-done.8
  10.2 0.1 copy.43
  10.3 0.1 mul.87
  10.4 0.1 eq.30
  10.5 0.1 fusion.2
  10.6 0.2 select_reduce_fusion.1
  10.8 0.1 reshape.78
  10.8 0.1 copy.42
  10.9 0.0 copy-done.5
  10.9 0.0 copy-done.3
  11.0 0.0 copy-done.4
  11.1 0.0 copy-done.2
  11.1 0.0 copy-done.7
  11.1 2.3 %multiply_add_fusion = f32[8,4,128,128]{3,2,1,0:T(8,128)} fusion(f32[8,4,128,128]{3,2,1,0:T(8,128)S(1)} %copy-done.2, f32[8,4,128]{2,1,0:T(4,128)S(1)} %get-tuple-element.31, f32[8,4,128]{2,1,0:T(4,128)S(1)} %get-tuple-element.32, f32[8,4,128]{2,1,0:T(4,128)S(1)} %get-tuple-element.30, f32[8,4,128]{2,1,0:T(4,128)S(1)} %get-tuple-element.33, f32[4]{0:T(128)S(1)} %copy-done.7), kind=kLoop, calls=%fused_computation | loop fusion | flops 3145728 | bytes 4259856 | tf_op jit(solution)/shard_map/add | solution.py:240
  13.3 0.0 copy-start.1
  13.3 0.1 select_reduce_fusion
  13.4 1.8 %all-to-all-done = bf16[8,16,512]{2,1,0:T(8,128)(2,1)S(1)} async-done(((bf16[8,16,512]{2,1,0:T(8,128)(2,1)}), bf16[8,16,512]{2,1,0:T(8,128)(2,1)S(1)}, u32[]{:S(2)}, u32[]{:S(2)}) %all-to-all-start) | async-done | bytes 131104 | tf_op jit(solution)/shard_map/all_to_all | solution.py:234
  15.2 0.0 copy-done
  15.2 0.3 fusion
  15.5 14.6 %all_to_all.20 = bf16[16,8,768]{2,1,0:T(8,128)(2,1)S(1)} all-to-all(bf16[16,8,768]{2,1,0:T(8,128)(2,1)S(1)} %fusion), channel_id=1, replica_groups=mesh['grp'=8,'head'=16] {'head'}, dimensions={0} | all-to-all | bytes 393216 | tf_op jit(solution)/shard_map/all_to_all | solution.py:269
  30.1 0.2 convolution_convert_fusion.1
  30.4 0.2 broadcast_in_dim.5
  30.6 18.3 %all_to_all.21.rows_ref = bf16[128,2,768]{2,1,0:T(2,128)(2,1)S(1)} all-to-all(bf16[128,2,768]{2,1,0:T(2,128)(2,1)S(1)} %bitcast.40), channel_id=1, replica_groups=mesh['grp'=8,'head'=16] {'grp','head'}, dimensions={0} | all-to-all | bytes 786432 | tf_op jit(solution)/shard_map/all_to_all | solution.py:283
  48.9 0.0 copy-done.1
  48.9 8.2 %experts.1 = bf16[128,2,768]{2,1,0:T(2,128)(2,1)S(1)} custom-call(bf16[128,2,768]{2,1,0:T(2,128)(2,1)S(1)} %all_to_all.21.rows_ref, f32[1,6144]{1,0:T(1,128)S(1)} %bitcast.36, bf16[576,6144]{1,0:T(8,128)(2,1)} %bitcast.37, bf16[576,6144]{1,0:T(8,128)(2,1)} %bitcast.38, bf16[576,6144]{1,0:T(8,128)(2,1)} %bitcast.39), custom_call_target="tpu_custom_call" | custom-call | flops 679477248 | bytes 21233664 | tf_op jit(solution)/shard_map/experts/pallas_call | solution.py:188
  57.1 16.6 %all_to_all.22 = bf16[128,2,768]{2,1,0:T(2,128)(2,1)S(1)} all-to-all(bf16[128,2,768]{2,1,0:T(2,128)(2,1)S(1)} %experts.1), channel_id=1, replica_groups=mesh['grp'=8,'head'=16] {'grp','head'}, dimensions={0} | all-to-all | bytes 786432 | tf_op jit(solution)/shard_map/all_to_all | solution.py:291
  73.7 0.1 reshape.90
  73.9 0.2 fusion.1
  74.0 0.6 reshape.83
  (11 shorter events, 0.2 us)
Async XLA Ops:
  0.6 14.5 %copy-start = (bf16[512,768]{1,0:T(8,128)(2,1)S(1)}, bf16[512,768]{1,0:T(8,128)(2,1)}, u32[]{:S(2)}) copy-start(bf16[512,768]{1,0:T(8,128)(2,1)} %param.20) | copy-start | bytes 2359300
  0.6 10.4 %copy-start.2 = (f32[8,4,128,128]{3,2,1,0:T(8,128)S(1)}, f32[8,4,128,128]{3,2,1,0:T(8,128)}, u32[]{:S(2)}) copy-start(f32[8,4,128,128]{3,2,1,0:T(8,128)} %states_ref.1) | copy-start | bytes 6291460
  0.7 10.4 %copy-start.7 = (f32[4]{0:T(128)S(1)}, f32[4]{0:T(128)}, u32[]{:S(2)}) copy-start(f32[4]{0:T(128)} %decay_in.1) | copy-start | bytes 52
  0.7 10.3 %copy-start.4 = (bf16[8,2,512]{2,1,0:T(2,128)(2,1)S(1)}, bf16[8,2,512]{2,1,0:T(2,128)(2,1)}, u32[]{:S(2)}) copy-start(bf16[8,2,512]{2,1,0:T(2,128)(2,1)} %value_in.1) | copy-start | bytes 49156
  0.7 10.3 %copy-start.3 = (bf16[8,2,512]{2,1,0:T(2,128)(2,1)S(1)}, bf16[8,2,512]{2,1,0:T(2,128)(2,1)}, u32[]{:S(2)}) copy-start(bf16[8,2,512]{2,1,0:T(2,128)(2,1)} %key_in.1) | copy-start | bytes 49156
  0.7 9.5 %copy-start.8 = (f32[4,2,2]{0,2,1:T(2,128)S(1)}, f32[4,2,2]{0,2,1:T(2,128)}, u32[]{:S(2)}) copy-start(f32[4,2,2]{0,2,1:T(2,128)} %param.27) | copy-start | bytes 196
  0.7 9.2 %copy-start.6 = (s32[4,2,2]{0,2,1:T(2,128)S(1)}, s32[4,2,2]{0,2,1:T(2,128)}, u32[]{:S(2)}) copy-start(s32[4,2,2]{0,2,1:T(2,128)} %param.26) | copy-start | bytes 196
  0.7 10.2 %copy-start.5 = (bf16[4,2,768]{2,1,0:T(2,128)(2,1)S(1)}, bf16[4,2,768]{2,1,0:T(2,128)(2,1)}, u32[]{:S(2)}) copy-start(bf16[4,2,768]{2,1,0:T(2,128)(2,1)} %param.21) | copy-start | bytes 36868
  4.1 11.1 %all-to-all-start = ((bf16[8,16,512]{2,1,0:T(8,128)(2,1)}), bf16[8,16,512]{2,1,0:T(8,128)(2,1)S(1)}, u32[]{:S(2)}, u32[]{:S(2)}) async-start(bf16[8,16,512]{2,1,0:T(8,128)(2,1)} %readouts.1), calls=%async_computation | async-start | bytes 262144 | tf_op jit(solution)/shard_map/all_to_all | solution.py:234
  13.3 35.6 %copy-start.1 = (f32[6144]{0:T(1024)S(1)}, f32[6144]{0:T(1024)}, u32[]{:S(2)}) copy-start(f32[6144]{0:T(1024)} %param.22) | copy-start | bytes 73732

commit v3 on v2

v3 whole, which is shorter than its diff:
```python
import jax
import jax.numpy as jnp
from jax import lax
from jax.experimental import pallas as pl
from jax.experimental.pallas import tpu as pltpu
from jax.sharding import PartitionSpec as P

CAP = 2
PLACES = (0, 1, 3, 2)
FIRST_HEAD = 11
FIRST_PLACE = 3
HIDDEN_STEPS = 4
DOWN_STEPS = 4
AHEAD = 4


EPSILON = 1e-06


def in_hbm(array):
    return pltpu.with_memory_space_constraint(array, pltpu.HBM)


def heads_in_order(count):
    return [FIRST_HEAD] + [head for head in range(count) if head != FIRST_HEAD]


def places_in_order(count):
    return [FIRST_PLACE] + [place for place in range(count) if place != FIRST_PLACE]


ROWS_CONTRACT = (((1,), (1,)), ((), ()))


def attend_kernel(
    query_in, key_in, value_in, decay_in, gain_in, routes_in, weights_in, stream_in, ffn_gain_in, states_in,
    out_ref, picker_ref, combiner_ref, stream_out, ffn_gain_out, held, left, right, faded_twice,
    query_ref, key_ref, value_ref, decay_ref, gain_ref, routes_ref, weights_ref, stream_ref, read, rows, small_sems, in_sems,
):
    requests, positions, _ = query_ref.shape
    heads, size = held.shape[1], held.shape[2]
    pairs = (
        (query_in, query_ref),
        (key_in, key_ref),
        (value_in, value_ref),
        (decay_in, decay_ref),
        (gain_in, gain_ref),
        (routes_in, routes_ref),
        (weights_in, weights_ref),
        (stream_in, stream_ref),
        (ffn_gain_in, ffn_gain_out),
    )
    small = [
        pltpu.make_async_copy(source, target, small_sems.at[index]) for index, (source, target) in enumerate(pairs)
    ]
    arriving = [
        pltpu.make_async_copy(states_in.at[request], held.at[request], in_sems.at[request])
        for request in range(requests)
    ]
    arriving[0].start()
    for copy in small[:4]:
        copy.start()
    for copy in arriving[1:]:
        copy.start()
    for copy in small[4:]:
        copy.start()
    for copy in small[:4]:
        copy.wait()

    first_part, own_part = [], []
    for head in range(heads):
        columns = slice(head * size, (head + 1) * size)
        query = query_ref[:, :, columns].astype(jnp.float32)
        keys = key_ref[:, :, columns].astype(jnp.float32)
        values = value_ref[:, :, columns].astype(jnp.float32)
        first_key, first_value = keys[:, 0:1, :], values[:, 0:1, :]
        first_part.append(jnp.sum(query * first_key, axis=2, keepdims=True) * first_value)
        own_part.append(jnp.sum(query * keys, axis=2, keepdims=True) * values)
        faded = decay_ref[head] * first_value
        faded_twice[:, columns] = jnp.full((1, size), decay_ref[head] * decay_ref[head], jnp.float32)
        high = faded.astype(jnp.bfloat16).astype(jnp.float32)
        middle = (faded - high).astype(jnp.bfloat16).astype(jnp.float32)
        left[:, :, columns] = jnp.concatenate([first_key, first_key, first_key, keys[:, 1:2, :]], axis=1)
        right[:, :, columns] = jnp.concatenate([high, middle, faded - high - middle, values[:, 1:2, :]], axis=1)

    for request in range(requests):
        arriving[request].wait()
        for head in range(heads):
            columns = slice(head * size, (head + 1) * size)
            state = held[request, head]
            high = state.astype(jnp.bfloat16)
            low = (state - high.astype(jnp.float32)).astype(jnp.bfloat16)
            query = query_ref[request, :, columns]
            read[request, :, columns] = jnp.dot(
                jnp.concatenate([query, query], axis=1),
                jnp.concatenate([high, low], axis=0),
                preferred_element_type=jnp.float32,
            )

    for copy in small[4:]:
        copy.wait()
    first = lax.broadcasted_iota(jnp.int32, (requests, positions, size), 1) == 0
    for head in range(heads):
        columns = slice(head * size, (head + 1) * size)
        decay = decay_ref[head]
        once = decay * read[:, :, columns] + first_part[head]
        readout = jnp.where(first, once, decay * once + own_part[head])
        scaled = (
            readout
            * lax.rsqrt(jnp.mean(readout * readout, axis=2, keepdims=True) + EPSILON)
            * gain_ref[0:1, columns][None]
        )
        for request in range(requests):
            rows[request * positions : (request + 1) * positions, columns] = scaled[request]
    out_ref[...] = rows[...].astype(jnp.bfloat16)

    token_count, choices = picker_ref.shape[1], routes_ref.shape[1]
    chosen, weights = [], []
    for token in range(token_count):
        for choice in range(choices):
            place = (token % positions, choice, token // positions)
            chosen.append(routes_ref[place])
            weights.append(weights_ref[place])
    slot_down = lax.broadcasted_iota(jnp.int32, picker_ref.shape, 0)
    token_across = lax.broadcasted_iota(jnp.int32, picker_ref.shape, 1)
    token_down = lax.broadcasted_iota(jnp.int32, combiner_ref.shape, 0)
    slot_across = lax.broadcasted_iota(jnp.int32, combiner_ref.shape, 1)
    picker = jnp.zeros(picker_ref.shape, jnp.float32)
    combiner = jnp.zeros(combiner_ref.shape, jnp.float32)
    for index, expert in enumerate(chosen):
        position = jnp.where(expert == FIRST_HEAD, 0, expert + (expert < FIRST_HEAD).astype(jnp.int32))
        slot = position * CAP
        for earlier in chosen[:index]:
            slot = slot + (earlier == expert).astype(jnp.int32)
        token = index // choices
        picker = jnp.where((slot_down == slot) & (token_across == token), 1.0, picker)
        combiner = jnp.where((slot_across == slot) & (token_down == token), weights[index], combiner)
    picker_ref[...] = picker.astype(jnp.bfloat16)
    combiner_ref[...] = combiner
    stream_out[...] = stream_ref[...].astype(jnp.float32).reshape(stream_out.shape)


def attend(
    query_in, key_in, value_in, decay_rate, attn_gain, routes, route_weights, stream_in, ffn_gain, states, slots
):
    requests, positions, width = query_in.shape
    tokens = stream_in.shape[0] * stream_in.shape[1]
    routes, route_weights = (jnp.transpose(array, (1, 2, 0)) for array in (routes, route_weights))
    vmem = pl.BlockSpec(memory_space=pltpu.VMEM)
    anywhere = pl.BlockSpec(memory_space=pl.ANY)
    inputs = (
        query_in, key_in, value_in, decay_rate, attn_gain.reshape(1, width), routes, route_weights, stream_in,
        ffn_gain.reshape(1, -1), states,
    )
    return pl.pallas_call(
        attend_kernel,
        out_shape=[
            pltpu.VMEM((requests * positions, width), jnp.bfloat16),
            pltpu.VMEM((slots, tokens), jnp.bfloat16),
            pltpu.VMEM((tokens, slots), jnp.float32),
            pltpu.VMEM((tokens, stream_in.shape[2]), jnp.float32),
            pltpu.VMEM((1, ffn_gain.shape[0]), jnp.float32),
            pltpu.VMEM(states.shape, jnp.float32),
            pltpu.VMEM((requests, 4, width), jnp.float32),
            pltpu.VMEM((requests, 4, width), jnp.float32),
            pltpu.VMEM((1, width), jnp.float32),
        ],
        in_specs=[anywhere] * len(inputs),
        out_specs=[vmem] * 9,
        scratch_shapes=[
            pltpu.VMEM(query_in.shape, jnp.bfloat16),
            pltpu.VMEM(query_in.shape, jnp.bfloat16),
            pltpu.VMEM(query_in.shape, jnp.bfloat16),
            pltpu.SMEM(decay_rate.shape, jnp.float32),
            pltpu.VMEM((1, width), jnp.float32),
            pltpu.SMEM(routes.shape, jnp.int32),
            pltpu.SMEM(route_weights.shape, jnp.float32),
            pltpu.VMEM(stream_in.shape, jnp.bfloat16),
            pltpu.VMEM(query_in.shape, jnp.float32),
            pltpu.VMEM((requests * positions, width), jnp.float32),
            pltpu.SemaphoreType.DMA((9,)),
            pltpu.SemaphoreType.DMA((requests,)),
        ],
        compiler_params=pltpu.CompilerParams(vmem_limit_bytes=32 * 2**20),
        cost_estimate=pl.CostEstimate(flops=10**7, bytes_accessed=states.size * 4, transcendentals=0),
        name="attend",
    )(*(in_hbm(array) for array in inputs))


def project_kernel(place_ref, own_ref, second_ref, third_ref, fourth_ref, weights_ref, out_ref, everyone):
    place = place_ref[0]
    rows = own_ref.shape[0]
    blocks, each, _ = out_ref.shape
    for index, ref in zip(PLACES, (own_ref, second_ref, third_ref, fourth_ref)):
        everyone[pl.ds(pl.multiple_of((place ^ index) * rows, rows), rows), :] = ref[...]
    partial = jnp.dot(everyone[...], weights_ref[...], preferred_element_type=jnp.float32).astype(jnp.bfloat16)
    for position, block in enumerate(heads_in_order(blocks)):
        out_ref[position] = partial[block * each : (block + 1) * each]


def project(place, gathered, weights, blocks):
    rows = len(gathered) * gathered[0].shape[0]
    vmem = pl.BlockSpec(memory_space=pltpu.VMEM)
    return pl.pallas_call(
        project_kernel,
        out_shape=jax.ShapeDtypeStruct((blocks, rows // blocks, weights.shape[1]), jnp.bfloat16),
        in_specs=[pl.BlockSpec(memory_space=pltpu.SMEM)] + [vmem] * 5,
        out_specs=vmem,
        scratch_shapes=[pltpu.VMEM((rows, weights.shape[0]), jnp.bfloat16)],
        compiler_params=pltpu.CompilerParams(vmem_limit_bytes=8 * 2**20),
        cost_estimate=pl.CostEstimate(flops=2 * rows * weights.size, bytes_accessed=2 * weights.size, transcendentals=0),
        name="project",
    )(place, *gathered, weights)


def update_kernel(states_ref, left_ref, right_ref, faded_ref, states_out, updated, sems):
    requests, heads, size, _ = states_ref.shape
    leaving = []
    for request in range(requests):
        for head in range(heads):
            columns = slice(head * size, (head + 1) * size)
            added = lax.dot_general(
                left_ref[request, :, columns].astype(jnp.bfloat16),
                right_ref[request, :, columns].astype(jnp.bfloat16),
                (((0,), (0,)), ((), ())),
                preferred_element_type=jnp.float32,
            )
            updated[request, head] = faded_ref[:, columns] * states_ref[request, head] + added
        leaving.append(pltpu.make_async_copy(updated.at[request], states_out.at[request], sems.at[request]))
        leaving[-1].start()
    for copy in leaving:
        copy.wait()


def update(states, left, right, faded_twice):
    vmem = pl.BlockSpec(memory_space=pltpu.VMEM)
    return pl.pallas_call(
        update_kernel,
        out_shape=pltpu.HBM(states.shape, jnp.float32),
        in_specs=[vmem] * 4,
        out_specs=pl.BlockSpec(memory_space=pl.ANY),
        scratch_shapes=[pltpu.VMEM(states.shape, jnp.float32), pltpu.SemaphoreType.DMA((states.shape[0],))],
        compiler_params=pltpu.CompilerParams(vmem_limit_bytes=16 * 2**20),
        cost_estimate=pl.CostEstimate(flops=10**7, bytes_accessed=states.size * 4, transcendentals=0),
        name="update",
    )(states, left, right, faded_twice)


def experts_kernel(
    core_ref, own_ref, partner_ref, gain_ref, gate_in, up_in, down_in, out_ref,
    normed, gate_ref, up_ref, down_ref, activated, sems,
):
    hidden, width = gate_in.shape
    columns = own_ref.shape[2]
    shards = width // columns
    places = places_in_order(shards // 2)
    blocks = own_ref.shape[0] // len(places)
    rows = blocks * own_ref.shape[1]
    tile = hidden // HIDDEN_STEPS
    wide = shards // DOWN_STEPS
    steps = HIDDEN_STEPS + DOWN_STEPS

    def copies(step):
        if step < HIDDEN_STEPS:
            cut = pl.ds(step * tile, tile)
            parts = ((gate_in.at[cut], gate_ref.at[cut]), (up_in.at[cut], up_ref.at[cut]))
        else:
            cut = pl.ds((step - HIDDEN_STEPS) * wide * columns, wide * columns)
            halves = (pl.ds(0, hidden // 2), pl.ds(hidden // 2, hidden // 2))
            parts = [(down_in.at[half, cut], down_ref.at[half, cut]) for half in halves]
        return [
            pltpu.make_async_copy(source, target, sems.at[step, index])
            for index, (source, target) in enumerate(parts)
        ]

    def begin(step):
        if step < steps:
            for copy in copies(step):
                copy.start()

    def finish(step):
        for copy in copies(step):
            copy.wait()
        begin(step + AHEAD)

    for step in range(AHEAD):
        begin(step)
    core = core_ref[0]
    squares = jnp.zeros((rows, 1), jnp.float32)
    for ref, side in ((own_ref, core), (partner_ref, 1 - core)):
        for index, place in enumerate(places):
            arrived = ref[index * blocks : (index + 1) * blocks].reshape(rows, columns)
            normed[:, pl.ds(pl.multiple_of((2 * place + side) * columns, 128), columns)] = arrived
            arrived = arrived.astype(jnp.float32)
            squares = squares + jnp.sum(arrived * arrived, axis=1, keepdims=True)
    scale = lax.rsqrt(squares / width + EPSILON)
    for shard in range(shards):
        cut = slice(shard * columns, (shard + 1) * columns)
        normed[:, cut] = (normed[:, cut].astype(jnp.float32) * scale * gain_ref[:, cut]).astype(jnp.bfloat16)
    for step in range(HIDDEN_STEPS):
        finish(step)
        cut = slice(step * tile, (step + 1) * tile)
        gate = lax.dot_general(gate_ref[cut], normed[...], ROWS_CONTRACT, preferred_element_type=jnp.float32)
        upward = lax.dot_general(up_ref[cut], normed[...], ROWS_CONTRACT, preferred_element_type=jnp.float32)
        activated[cut, :] = (gate / (1.0 + jnp.exp(-gate)) * upward).astype(jnp.bfloat16)
    for step in range(DOWN_STEPS):
        finish(HIDDEN_STEPS + step)
        for shard in range(step * wide, (step + 1) * wide):
            produced = lax.dot_general(
                activated[...],
                down_ref[:, shard * columns : (shard + 1) * columns],
                (((0,), (0,)), ((), ())),
                preferred_element_type=jnp.float32,
            )
            out_ref[shard * blocks : (shard + 1) * blocks] = produced.astype(jnp.bfloat16).reshape(
                blocks, rows // blocks, columns
            )


def expert_rows(core, own, partner, gain, gate, up, down):
    hidden, width = gate.shape
    count, slots, columns = own.shape
    rows = 2 * count * slots * columns // width
    vmem = pl.BlockSpec(memory_space=pltpu.VMEM)
    hbm = pl.BlockSpec(memory_space=pl.ANY)
    return pl.pallas_call(
        experts_kernel,
        out_shape=jax.ShapeDtypeStruct((2 * count, slots, columns), jnp.bfloat16),
        in_specs=[pl.BlockSpec(memory_space=pltpu.SMEM), vmem, vmem, vmem, hbm, hbm, hbm],
        out_specs=vmem,
        scratch_shapes=[
            pltpu.VMEM((rows, width), jnp.bfloat16),
            pltpu.VMEM((hidden, width), jnp.bfloat16),
            pltpu.VMEM((hidden, width), jnp.bfloat16),
            pltpu.VMEM((hidden, width), jnp.bfloat16),
            pltpu.VMEM((hidden, rows), jnp.bfloat16),
            pltpu.SemaphoreType.DMA((HIDDEN_STEPS + DOWN_STEPS, 2)),
        ],
        compiler_params=pltpu.CompilerParams(vmem_limit_bytes=48 * 2**20),
        cost_estimate=pl.CostEstimate(flops=6 * rows * hidden * width, bytes_accessed=6 * hidden * width, transcendentals=0),
        name="experts",
    )(core, own, partner, gain, in_hbm(gate), in_hbm(up), in_hbm(down))


def body(
    query_in,
    key_in,
    value_in,
    decay_rate,
    states,
    attn_gain,
    out_proj,
    stream_in,
    ffn_gain,
    expert_gate,
    expert_up,
    expert_down,
    routes,
    route_weights,
):
    requests_here, positions, width_here = query_in.shape
    groups = lax.axis_size("grp")
    heads = lax.axis_size("head")
    tokens_here = stream_in.shape[0] * positions
    columns = stream_in.shape[2]
    experts = heads * expert_gate.shape[0]
    slots_all = experts * CAP
    attended, picker, combiner, stream, gain, *state_parts = attend(
        query_in, key_in, value_in, decay_rate, attn_gain, routes, route_weights, stream_in, ffn_gain, states, slots_all
    )
    place = lax.axis_index("grp")
    partner = lax.ppermute(attended, "grp", [(one, one ^ 1) for one in range(groups)])
    pair = jnp.where(
        place % 2 == 0, jnp.concatenate([attended, partner]), jnp.concatenate([partner, attended])
    )
    gathered = [pair] + [
        lax.ppermute(pair, "grp", [(one, one ^ (2 * step)) for one in range(groups)]) for step in PLACES[1:]
    ]
    gathered, memory_state = lax.optimization_barrier((gathered, update(*state_parts)))
    partial_sums = project((place // 2).astype(jnp.int32).reshape(1), gathered, out_proj, heads)
    shares = lax.all_to_all(
        partial_sums,
        "head",
        split_axis=0,
        concat_axis=0,
        axis_index_groups=[heads_in_order(heads)],
        tiled=True,
    )
    mixed = jnp.sum(shares.astype(jnp.float32), axis=0)
    residual = (stream + mixed).astype(jnp.bfloat16)
    slot_rows = (
        jnp.dot(picker, residual, preferred_element_type=jnp.float32)
        .astype(jnp.bfloat16)
        .reshape(1, experts, CAP, columns)
    )
    in_order = heads_in_order(heads)
    own = lax.all_to_all(
        jnp.broadcast_to(slot_rows, (groups // 2, experts, CAP, columns)).reshape(-1, CAP, columns),
        ("grp", "head"),
        split_axis=0,
        concat_axis=0,
        axis_index_groups=[
            [(2 * one + core) * heads + head for one in places_in_order(groups // 2) for head in in_order]
            for core in range(2)
        ],
        tiled=True,
    )
    outgoing = expert_rows(
        (place % 2).astype(jnp.int32).reshape(1),
        own,
        lax.ppermute(own, "grp", [(one, one ^ 1) for one in range(groups)]),
        gain,
        expert_gate[0],
        expert_up[0],
        expert_down[0],
    )
    returned = lax.all_to_all(
        outgoing,
        ("grp", "head"),
        split_axis=0,
        concat_axis=0,
        axis_index_groups=[[one * heads + head for one in range(groups) for head in in_order]],
        tiled=True,
    ).reshape(groups, slots_all, columns)
    moe = jnp.dot(
        combiner,
        jnp.sum(returned.astype(jnp.float32), axis=0),
        precision=lax.Precision.HIGHEST,
        preferred_element_type=jnp.float32,
    )
    stream_out = (residual.astype(jnp.float32) + moe).astype(jnp.bfloat16).reshape(stream_in.shape)
    return (stream_out, memory_state)


def solution(mesh):
    return jax.shard_map(
        body,
        mesh=mesh,
        in_specs=(
            P("grp", None, "head"),
            P("grp", None, "head"),
            P("grp", None, "head"),
            P("head"),
            P("grp", "head", None, None),
            P("head"),
            P("head", "grp"),
            P("head", None, "grp"),
            P(),
            P("head", "grp", None),
            P("head", "grp", None),
            P("head", "grp", None),
            P("head", None, None),
            P("head", None, None),
        ),
        out_specs=(P("head", None, "grp"), P("grp", "head", None, None)),
        check_vma=False,
    )
```

time: 74.9 us -> 72.9 us (0.973)
  blocking collectives: 49.5 us -> 44.8 us
  starting transfers between devices: 5.81 us -> 9.55 us
  other arithmetic: 2.74 us -> 0.09 us
  waiting for transfers between devices: 1.75 us -> 3.4 us
  Pallas kernels: 11.6 us -> 12.9 us
  local copies, waits for them, and re-layouts: 1.77 us -> 0.86 us
    ppermute x0 -> x5, starting transfers between devices: none -> 9.55 us  [the longest x1 4.28 us: body(): lax.ppermute(own, 'grp', [(one, one ^ 1) for one in range(groups)])]
    all_to_all x1 -> x0, starting transfers between devices: 5.81 us -> none  [body(): lax.all_to_all(attended, 'grp', split_axis=0, concat_axis=0, tiled=True)]
    all_to_all x3, blocking collectives: 49.5 us -> 44.8 us  [the longest x1 19.4 us: body(): lax.all_to_all(outgoing, ('grp', 'head'), split_axis=0, concat_axis=0, ax...]
    ppermute x0 -> x5, waiting for transfers between devices: none -> 3.4 us  [the longest x3 1.49 us: body(): lax.ppermute(pair, 'grp', [(one, one ^ 2 * step) for one in range(groups)])]
    add x2 -> x0, other arithmetic: 2.28 us -> none  [the longest x1 2.27 us: body(): decay[None, :, None, None] * memory_state]
    all_to_all x1 -> x0, waiting for transfers between devices: 1.75 us -> none  [body(): lax.all_to_all(attended, 'grp', split_axis=0, concat_axis=0, tiled=True)]
    pallas_call x2 -> x4, Pallas kernels: 11.6 us -> 12.9 us  [the longest x1 8.27 us: expert_rows(): pl.pallas_call(experts_kernel, out_shape=jax.ShapeDtypeStruct((2 * count,...]
  transfers between devices with their start and end apart: 1 -> 5, of which waited for: 1 -> 3; matrix products, arithmetic and copies ran while one was open for 5% -> 0% of each run, Pallas kernels for 0% -> 2%
where the time goes in v3:
time: 72.9 us; the launch traced here: 72.7 us
  blocking collectives  44.8 us (61%)
  Pallas kernels  12.9 us (18%)
  starting transfers between devices  9.55 us (13%)
  waiting for transfers between devices  3.4 us (5%)
  local copies, waits for them, and re-layouts  0.86 us (1%)
  between operations  0.74 us (1%)
    all_to_all x1, blocking collectives, body(): lax.all_to_all(outgoing, ('grp', 'head'), split_axis=0, concat_axis=0, ax...  19.4 us
    all_to_all x1, blocking collectives, body(): lax.all_to_all(jnp.broadcast_to(slot_rows, (groups // 2, experts, CAP, co...  13.3 us
    all_to_all x1, blocking collectives, body(): lax.all_to_all(partial_sums, 'head', split_axis=0, concat_axis=0, axis_in...  12.1 us
    pallas_call x1, Pallas kernels, expert_rows(): pl.pallas_call(experts_kernel, out_shape=jax.ShapeDtypeStruct((2 * count,...  8.27 us
    ppermute x1, starting transfers between devices, body(): lax.ppermute(own, 'grp', [(one, one ^ 1) for one in range(groups)])  4.28 us
    ppermute x3, starting transfers between devices, body(): lax.ppermute(pair, 'grp', [(one, one ^ 2 * step) for one in range(groups)])  3.76 us
    pallas_call x1, Pallas kernels, attend(): pl.pallas_call(attend_kernel, out_shape=[pltpu.VMEM((requests * positions...  2.78 us
    pallas_call x1, Pallas kernels, update(): pl.pallas_call(update_kernel, out_shape=pltpu.HBM(states.shape, jnp.float...  1.61 us
  transfers between devices with their start and end apart: 5, of which 3 were waited for; matrix products, arithmetic and copies ran while one was open for 0% of the time, Pallas kernels for 2%

profile of v3, /device:TPU:1, one launch (start us, length us, event | category | flops | bytes accessed | tf_op | source)
XLA Modules:
  0.0 72.7 jit_solution(2281406907809297548)
XLA Ops:
  0.6 0.0 copy-start
  0.6 2.8 %attend.1 = (bf16[16,512]{1,0:T(8,128)(2,1)S(1)}, bf16[32,8]{1,0:T(8,128)(2,1)S(1)}, f32[8,32]{1,0:T(8,128)S(1)}, f32[8,768]{1,0:T(8,128)S(1)}, f32[1,6144]{1,0:...) custom-call(bf16[8,2,512]{2,1,0:T(2,128)(2,1)} %query_in.1, ...), custom_call_target="tpu_custom_call" | custom-call | flops 10000000 | bytes 2097152 | tf_op jit(solution)/shard_map/attend/pallas_call | solution.py:155
  3.4 1.5 %collective-permute-start = (bf16[16,512]{1,0:T(8,128)(2,1)S(1)}, bf16[16,512]{1,0:T(8,128)(2,1)S(1)}, u32[]{:S(2)}, u32[]{:S(2)}) collective-permute-start(bf16[16,512]{1,0:T(8,128)(2,1)S(1)} %get-tuple-element.17), channel_id=1, source_target_pairs={{0,16},{16,0},{32,48},{48,32},{64,80},{80,64},{96,112},{112,96},{1... | collective-permute-start | bytes 49160 | tf_op jit(solution)/shard_map/ppermute | solution.py:372
  4.9 0.8 %collective-permute-done = bf16[16,512]{1,0:T(8,128)(2,1)S(1)} collective-permute-done((bf16[16,512]{1,0:T(8,128)(2,1)S(1)}, bf16[16,512]{1,0:T(8,128)(2,1)S(1)}, u32[]{:S(2)}, u32[]{:S(2)}) %collective-permute-start) | collective-permute-done | bytes 16416 | tf_op jit(solution)/shard_map/ppermute | solution.py:372
  5.8 2.9 %collective-permute-start.3 = (bf16[32,512]{1,0:T(8,128)(2,1)S(1)}, bf16[32,512]{1,0:T(8,128)(2,1)S(1)}, u32[]{:S(2)}, u32[]{:S(2)}) collective-permute-start(bf16[32,512]{1,0:T(8,128)(2,1)S(1)} %maximum_select_fusion.own_ref), channel_id=1, source_target_pairs={{0,64},{16,80},{32,96},{48,112},{64,0},{80,16},{96,32},{112,48},{1... | collective-permute-start | bytes 98312 | tf_op jit(solution)/shard_map/ppermute | solution.py:377
  8.7 0.9 %collective-permute-start.2 = (bf16[32,512]{1,0:T(8,128)(2,1)S(1)}, bf16[32,512]{1,0:T(8,128)(2,1)S(1)}, u32[]{:S(2)}, u32[]{:S(2)}) collective-permute-start(bf16[32,512]{1,0:T(8,128)(2,1)S(1)} %maximum_select_fusion.own_ref), channel_id=1, source_target_pairs={{0,96},{16,112},{32,64},{48,80},{64,32},{80,48},{96,0},{112,16},{1... | collective-permute-start | bytes 98312 | tf_op jit(solution)/shard_map/ppermute | solution.py:377
  9.5 0.0 collective-permute-start.1
  9.5 1.6 %update.1 = f32[8,4,128,128]{3,2,1,0:T(8,128)} custom-call(f32[8,4,128,128]{3,2,1,0:T(8,128)S(1)} %get-tuple-element.18.states_ref, f32[8,4,512]{2,1,0:T(4,128)S(1)} %get-tuple-element.19.left_ref, f32[8,4,512]{2,1,0:T(4,128)S(1)} %get-tuple-element.20.right_ref, f32[1,512]{1,0:T(1,128)S(1)} %get-tuple-element.21.faded_ref), custom_call_target="tpu_custom_call" | custom-call | flops 10000000 | bytes 2097152 | tf_op jit(solution)/shard_map/update/pallas_call | solution.py:237
  11.2 0.0 collective-permute-done.3.fourth_ref
  11.2 1.5 %collective-permute-done.2.third_ref = bf16[32,512]{1,0:T(8,128)(2,1)S(1)} collective-permute-done((bf16[32,512]{1,0:T(8,128)(2,1)S(1)}, bf16[32,512]{1,0:T(8,128)(2,1)S(1)}, u32[]{:S(2)}, u32[]{:S(2)}) %collective-permute-start.2) | collective-permute-done | bytes 32800 | tf_op jit(solution)/shard_map/ppermute | solution.py:377
  12.7 0.0 collective-permute-done.1.second_ref
  12.7 0.0 copy-done
  12.7 0.3 project.1
  12.9 12.1 %all_to_all.15 = bf16[16,8,768]{2,1,0:T(8,128)(2,1)S(1)} all-to-all(bf16[16,8,768]{2,1,0:T(8,128)(2,1)S(1)} %project.1), channel_id=1, replica_groups={{11,0,1,2,3,4,5,6,7,8,9,10,12,13,14,15},{27,16,17,18,19,20,21,22,23,24,..., dimensions={0} | all-to-all | bytes 393216 | tf_op jit(solution)/shard_map/all_to_all | solution.py:381
  25.1 0.1 convolution_convert_fusion
  25.3 0.1 broadcast_in_dim.8
  25.4 13.3 %all_to_all.16.own_ref = bf16[64,2,768]{2,1,0:T(2,128)(2,1)S(1)} all-to-all(bf16[64,2,768]{2,1,0:T(2,128)(2,1)S(1)} %bitcast.17), channel_id=1, replica_groups={{107,96,97,98,99,100,101,102,103,104,105,106,108,109,110,111,11,0,1,2,3..., dimensions={0} | all-to-all | bytes 393216 | tf_op jit(solution)/shard_map/all_to_all | solution.py:397
  38.7 4.3 %collective-permute-start.4 = (bf16[64,2,768]{2,1,0:T(2,128)(2,1)S(1)}, bf16[64,2,768]{2,1,0:T(2,128)(2,1)S(1)}, u32[]{:S(2)}, u32[]{:S(2)}) collective-permute-start(bf16[64,2,768]{2,1,0:T(2,128)(2,1)S(1)} %all_to_all.16.own_ref), channel_id=1, source_target_pairs={{0,16},{16,0},{32,48},{48,32},{64,80},{80,64},{96,112},{112,96},{1... | collective-permute-start | bytes 589832 | tf_op jit(solution)/shard_map/ppermute | solution.py:411
  43.0 1.1 %collective-permute-done.4.partner_ref = bf16[64,2,768]{2,1,0:T(2,128)(2,1)S(1)} collective-permute-done((bf16[64,2,768]{2,1,0:T(2,128)(2,1)S(1)}, bf16[64,2,768]{2,1,0:T(2,128)(2,1)S(1)}, u32[]{:S(2)}, u32[]{:S(2)}) %collective-permute-start.4) | collective-permute-done | bytes 196640 | tf_op jit(solution)/shard_map/ppermute | solution.py:411
  44.1 8.3 %experts.1 = bf16[128,2,768]{2,1,0:T(2,128)(2,1)S(1)} custom-call(s32[1]{0:T(128)} %bitcast.5.core_ref, bf16[64,2,768]{2,1,0:T(2,128)(2,1)S(1)} %all_to_all.16.own_ref, bf16[64,2,768]{2,1,0:T(2,128)(2,1)S(1)} %collective-permute-done.4.partner_ref, f32[1,6144]{1,0:T(1,128)S(1)} %get-tuple-element.28.gain_ref, bf16[576,6144]{1,0:T(8,128)(2,1)} %bitcast.14, ...), custom_call_target="tpu_custom_call" | custom-call | flops 679477248 | bytes 21233664 | tf_op jit(solution)/shard_map/experts/pallas_call | solution.py:326
  52.4 19.4 %all_to_all.17 = bf16[128,2,768]{2,1,0:T(2,128)(2,1)S(1)} all-to-all(bf16[128,2,768]{2,1,0:T(2,128)(2,1)S(1)} %experts.1), channel_id=1, replica_groups={{11,0,1,2,3,4,5,6,7,8,9,10,12,13,14,15,27,16,17,18,19,20,21,22,23,24,25..., dimensions={0} | all-to-all | bytes 786432 | tf_op jit(solution)/shard_map/all_to_all | solution.py:417
  71.7 0.1 reshape.33
  71.9 0.2 fusion
  72.1 0.6 reshape.32
  (5 shorter events, 0.1 us)
Async XLA Ops:
  0.6 12.0 %copy-start = (bf16[512,768]{1,0:T(8,128)(2,1)S(1)}, bf16[512,768]{1,0:T(8,128)(2,1)}, u32[]{:S(2)}) copy-start(bf16[512,768]{1,0:T(8,128)(2,1)} %weights_ref.1) | copy-start | bytes 2359300
  3.4 2.3 %collective-permute-start = (bf16[16,512]{1,0:T(8,128)(2,1)S(1)}, bf16[16,512]{1,0:T(8,128)(2,1)S(1)}, u32[]{:S(2)}, u32[]{:S(2)}) collective-permute-start(bf16[16,512]{1,0:T(8,128)(2,1)S(1)} %get-tuple-element.17), channel_id=1, source_target_pairs={{0,16},{16,0},{32,48},{48,32},{64,80},{80,64},{96,112},{112,96},{1... | collective-permute-start | bytes 49160 | tf_op jit(solution)/shard_map/ppermute | solution.py:372
  5.8 5.4 %collective-permute-start.3 = (bf16[32,512]{1,0:T(8,128)(2,1)S(1)}, bf16[32,512]{1,0:T(8,128)(2,1)S(1)}, u32[]{:S(2)}, u32[]{:S(2)}) collective-permute-start(bf16[32,512]{1,0:T(8,128)(2,1)S(1)} %maximum_select_fusion.own_ref), channel_id=1, source_target_pairs={{0,64},{16,80},{32,96},{48,112},{64,0},{80,16},{96,32},{112,48},{1... | collective-permute-start | bytes 98312 | tf_op jit(solution)/shard_map/ppermute | solution.py:377
  8.7 4.0 %collective-permute-start.2 = (bf16[32,512]{1,0:T(8,128)(2,1)S(1)}, bf16[32,512]{1,0:T(8,128)(2,1)S(1)}, u32[]{:S(2)}, u32[]{:S(2)}) collective-permute-start(bf16[32,512]{1,0:T(8,128)(2,1)S(1)} %maximum_select_fusion.own_ref), channel_id=1, source_target_pairs={{0,96},{16,112},{32,64},{48,80},{64,32},{80,48},{96,0},{112,16},{1... | collective-permute-start | bytes 98312 | tf_op jit(solution)/shard_map/ppermute | solution.py:377
  9.5 3.1 %collective-permute-start.1 = (bf16[32,512]{1,0:T(8,128)(2,1)S(1)}, bf16[32,512]{1,0:T(8,128)(2,1)S(1)}, u32[]{:S(2)}, u32[]{:S(2)}) collective-permute-start(bf16[32,512]{1,0:T(8,128)(2,1)S(1)} %maximum_select_fusion.own_ref), channel_id=1, source_target_pairs={{0,32},{16,48},{32,0},{48,16},{64,96},{80,112},{96,64},{112,80},{1... | collective-permute-start | bytes 98312 | tf_op jit(solution)/shard_map/ppermute | solution.py:377
  38.7 5.4 %collective-permute-start.4 = (bf16[64,2,768]{2,1,0:T(2,128)(2,1)S(1)}, bf16[64,2,768]{2,1,0:T(2,128)(2,1)S(1)}, u32[]{:S(2)}, u32[]{:S(2)}) collective-permute-start(bf16[64,2,768]{2,1,0:T(2,128)(2,1)S(1)} %all_to_all.16.own_ref), channel_id=1, source_target_pairs={{0,16},{16,0},{32,48},{48,32},{64,80},{80,64},{96,112},{112,96},{1... | collective-permute-start | bytes 589832 | tf_op jit(solution)/shard_map/ppermute | solution.py:411

commit v4 on v3

--- a/solution.py
+++ b/solution.py
@@ -7,10 +7,12 @@
 
 CAP = 2
 PLACES = (0, 1, 3, 2)
-FIRST_HEAD = 11
+LATE_HEAD = 15
+FIRST_HEAD = 15
 FIRST_PLACE = 3
 HIDDEN_STEPS = 4
-DOWN_STEPS = 4
+DOWN_WIDTHS = (3, 3, 2)
+TOGETHER = 2
 AHEAD = 4
 
 
@@ -21,8 +23,8 @@
     return pltpu.with_memory_space_constraint(array, pltpu.HBM)
 
 
-def heads_in_order(count):
-    return [FIRST_HEAD] + [head for head in range(count) if head != FIRST_HEAD]
+def heads_in_order(count, first=FIRST_HEAD):
+    return [first] + [head for head in range(count) if head != first]
 
 
 def places_in_order(count):
@@ -54,8 +56,10 @@
         pltpu.make_async_copy(source, target, small_sems.at[index]) for index, (source, target) in enumerate(pairs)
     ]
     arriving = [
-        pltpu.make_async_copy(states_in.at[request], held.at[request], in_sems.at[request])
-        for request in range(requests)
+        pltpu.make_async_copy(
+            states_in.at[pl.ds(start, TOGETHER)], held.at[pl.ds(start, TOGETHER)], in_sems.at[start // TOGETHER]
+        )
+        for start in range(0, requests, TOGETHER)
     ]
     arriving[0].start()
     for copy in small[:4]:
@@ -84,7 +88,8 @@
         right[:, :, columns] = jnp.concatenate([high, middle, faded - high - middle, values[:, 1:2, :]], axis=1)
 
     for request in range(requests):
-        arriving[request].wait()
+        if request % TOGETHER == 0:
+            arriving[request // TOGETHER].wait()
         for head in range(heads):
             columns = slice(head * size, (head + 1) * size)
             state = held[request, head]
@@ -194,7 +199,7 @@
     for index, ref in zip(PLACES, (own_ref, second_ref, third_ref, fourth_ref)):
         everyone[pl.ds(pl.multiple_of((place ^ index) * rows, rows), rows), :] = ref[...]
     partial = jnp.dot(everyone[...], weights_ref[...], preferred_element_type=jnp.float32).astype(jnp.bfloat16)
-    for position, block in enumerate(heads_in_order(blocks)):
+    for position, block in enumerate(heads_in_order(blocks, LATE_HEAD)):
         out_ref[position] = partial[block * each : (block + 1) * each]
 
 
@@ -257,17 +262,20 @@
     blocks = own_ref.shape[0] // len(places)
     rows = blocks * own_ref.shape[1]
     tile = hidden // HIDDEN_STEPS
-    wide = shards // DOWN_STEPS
-    steps = HIDDEN_STEPS + DOWN_STEPS
+    steps = HIDDEN_STEPS + len(DOWN_WIDTHS)
+
+    def down_shards(step):
+        start = sum(DOWN_WIDTHS[:step])
+        return range(start, start + DOWN_WIDTHS[step])
 
     def copies(step):
         if step < HIDDEN_STEPS:
             cut = pl.ds(step * tile, tile)
-            parts = ((gate_in.at[cut], gate_ref.at[cut]), (up_in.at[cut], up_ref.at[cut]))
+            parts = [(gate_in.at[cut], gate_ref.at[cut]), (up_in.at[cut], up_ref.at[cut])]
         else:
-            cut = pl.ds((step - HIDDEN_STEPS) * wide * columns, wide * columns)
-            halves = (pl.ds(0, hidden // 2), pl.ds(hidden // 2, hidden // 2))
-            parts = [(down_in.at[half, cut], down_ref.at[half, cut]) for half in halves]
+            here = down_shards(step - HIDDEN_STEPS)
+            cut = pl.ds(here.start * columns, len(here) * columns)
+            parts = [(down_in.at[:, cut], down_ref.at[:, cut])]
         return [
             pltpu.make_async_copy(source, target, sems.at[step, index])
             for index, (source, target) in enumerate(parts)
@@ -303,9 +311,9 @@
         gate = lax.dot_general(gate_ref[cut], normed[...], ROWS_CONTRACT, preferred_element_type=jnp.float32)
         upward = lax.dot_general(up_ref[cut], normed[...], ROWS_CONTRACT, preferred_element_type=jnp.float32)
         activated[cut, :] = (gate / (1.0 + jnp.exp(-gate)) * upward).astype(jnp.bfloat16)
-    for step in range(DOWN_STEPS):
+    for step in range(len(DOWN_WIDTHS)):
         finish(HIDDEN_STEPS + step)
-        for shard in range(step * wide, (step + 1) * wide):
+        for shard in down_shards(step):
             produced = lax.dot_general(
                 activated[...],
                 down_ref[:, shard * columns : (shard + 1) * columns],
@@ -334,7 +342,7 @@
             pltpu.VMEM((hidden, width), jnp.bfloat16),
             pltpu.VMEM((hidden, width), jnp.bfloat16),
             pltpu.VMEM((hidden, rows), jnp.bfloat16),
-            pltpu.SemaphoreType.DMA((HIDDEN_STEPS + DOWN_STEPS, 2)),
+            pltpu.SemaphoreType.DMA((HIDDEN_STEPS + len(DOWN_WIDTHS), 2)),
         ],
         compiler_params=pltpu.CompilerParams(vmem_limit_bytes=48 * 2**20),
         cost_estimate=pl.CostEstimate(flops=6 * rows * hidden * width, bytes_accessed=6 * hidden * width, transcendentals=0),
@@ -383,7 +391,7 @@
         "head",
         split_axis=0,
         concat_axis=0,
-        axis_index_groups=[heads_in_order(heads)],
+        axis_index_groups=[heads_in_order(heads, LATE_HEAD)],
         tiled=True,
     )
     mixed = jnp.sum(shares.astype(jnp.float32), axis=0)

time: 72.9 us -> 72.5 us (level)
  no operation moved by 1% of the time
where the time goes in v4:
time: 72.5 us; the launch traced here: 72.3 us
  blocking collectives  45.1 us (62%)
  Pallas kernels  12.5 us (17%)
  starting transfers between devices  9.37 us (13%)
  waiting for transfers between devices  3.4 us (5%)
  local copies, waits for them, and re-layouts  0.86 us (1%)
  between operations  0.74 us (1%)
    all_to_all x1, blocking collectives, body(): lax.all_to_all(outgoing, ('grp', 'head'), split_axis=0, concat_axis=0, ax...  19.1 us
    all_to_all x1, blocking collectives, body(): lax.all_to_all(jnp.broadcast_to(slot_rows, (groups // 2, experts, CAP, co...  13.5 us
    all_to_all x1, blocking collectives, body(): lax.all_to_all(partial_sums, 'head', split_axis=0, concat_axis=0, axis_in...  12.5 us
    pallas_call x1, Pallas kernels, expert_rows(): pl.pallas_call(experts_kernel, out_shape=jax.ShapeDtypeStruct((2 * count,...  8.15 us
    ppermute x1, starting transfers between devices, body(): lax.ppermute(own, 'grp', [(one, one ^ 1) for one in range(groups)])  4.11 us
    ppermute x3, starting transfers between devices, body(): lax.ppermute(pair, 'grp', [(one, one ^ 2 * step) for one in range(groups)])  3.76 us
    pallas_call x1, Pallas kernels, attend(): pl.pallas_call(attend_kernel, out_shape=[pltpu.VMEM((requests * positions...  2.42 us
    pallas_call x1, Pallas kernels, update(): pl.pallas_call(update_kernel, out_shape=pltpu.HBM(states.shape, jnp.float...  1.61 us
  transfers between devices with their start and end apart: 5, of which 3 were waited for; matrix products, arithmetic and copies ran while one was open for 0% of the time, Pallas kernels for 2%

profile of v4, /device:TPU:1, one launch (start us, length us, event | category | flops | bytes accessed | tf_op | source)
XLA Modules:
  0.0 72.3 jit_solution(3334228101292337626)
XLA Ops:
  0.6 0.0 copy-start
  0.6 2.4 %attend.1 = (bf16[16,512]{1,0:T(8,128)(2,1)S(1)}, bf16[32,8]{1,0:T(8,128)(2,1)S(1)}, f32[8,32]{1,0:T(8,128)S(1)}, f32[8,768]{1,0:T(8,128)S(1)}, f32[1,6144]{1,0:...) custom-call(bf16[8,2,512]{2,1,0:T(2,128)(2,1)} %query_in.1, ...), custom_call_target="tpu_custom_call" | custom-call | flops 10000000 | bytes 2097152 | tf_op jit(solution)/shard_map/attend/pallas_call | solution.py:160
  3.1 1.5 %collective-permute-start = (bf16[16,512]{1,0:T(8,128)(2,1)S(1)}, bf16[16,512]{1,0:T(8,128)(2,1)S(1)}, u32[]{:S(2)}, u32[]{:S(2)}) collective-permute-start(bf16[16,512]{1,0:T(8,128)(2,1)S(1)} %get-tuple-element.17), channel_id=1, source_target_pairs={{0,16},{16,0},{32,48},{48,32},{64,80},{80,64},{96,112},{112,96},{1... | collective-permute-start | bytes 49160 | tf_op jit(solution)/shard_map/ppermute | solution.py:380
  4.6 0.8 %collective-permute-done = bf16[16,512]{1,0:T(8,128)(2,1)S(1)} collective-permute-done((bf16[16,512]{1,0:T(8,128)(2,1)S(1)}, bf16[16,512]{1,0:T(8,128)(2,1)S(1)}, u32[]{:S(2)}, u32[]{:S(2)}) %collective-permute-start) | collective-permute-done | bytes 16416 | tf_op jit(solution)/shard_map/ppermute | solution.py:380
  5.4 2.9 %collective-permute-start.3 = (bf16[32,512]{1,0:T(8,128)(2,1)S(1)}, bf16[32,512]{1,0:T(8,128)(2,1)S(1)}, u32[]{:S(2)}, u32[]{:S(2)}) collective-permute-start(bf16[32,512]{1,0:T(8,128)(2,1)S(1)} %maximum_select_fusion.own_ref), channel_id=1, source_target_pairs={{0,64},{16,80},{32,96},{48,112},{64,0},{80,16},{96,32},{112,48},{1... | collective-permute-start | bytes 98312 | tf_op jit(solution)/shard_map/ppermute | solution.py:385
  8.3 0.9 %collective-permute-start.2 = (bf16[32,512]{1,0:T(8,128)(2,1)S(1)}, bf16[32,512]{1,0:T(8,128)(2,1)S(1)}, u32[]{:S(2)}, u32[]{:S(2)}) collective-permute-start(bf16[32,512]{1,0:T(8,128)(2,1)S(1)} %maximum_select_fusion.own_ref), channel_id=1, source_target_pairs={{0,96},{16,112},{32,64},{48,80},{64,32},{80,48},{96,0},{112,16},{1... | collective-permute-start | bytes 98312 | tf_op jit(solution)/shard_map/ppermute | solution.py:385
  9.2 0.0 collective-permute-start.1
  9.2 1.6 %update.1 = f32[8,4,128,128]{3,2,1,0:T(8,128)} custom-call(f32[8,4,128,128]{3,2,1,0:T(8,128)S(1)} %get-tuple-element.18.states_ref, f32[8,4,512]{2,1,0:T(4,128)S(1)} %get-tuple-element.19.left_ref, f32[8,4,512]{2,1,0:T(4,128)S(1)} %get-tuple-element.20.right_ref, f32[1,512]{1,0:T(1,128)S(1)} %get-tuple-element.21.faded_ref), custom_call_target="tpu_custom_call" | custom-call | flops 10000000 | bytes 2097152 | tf_op jit(solution)/shard_map/update/pallas_call | solution.py:242
  10.8 0.0 collective-permute-done.3.fourth_ref
  10.8 1.5 %collective-permute-done.2.third_ref = bf16[32,512]{1,0:T(8,128)(2,1)S(1)} collective-permute-done((bf16[32,512]{1,0:T(8,128)(2,1)S(1)}, bf16[32,512]{1,0:T(8,128)(2,1)S(1)}, u32[]{:S(2)}, u32[]{:S(2)}) %collective-permute-start.2) | collective-permute-done | bytes 32800 | tf_op jit(solution)/shard_map/ppermute | solution.py:385
  12.3 0.0 collective-permute-done.1.second_ref
  12.3 0.0 copy-done
  12.3 0.3 project.1
  12.6 12.5 %all_to_all.15 = bf16[16,8,768]{2,1,0:T(8,128)(2,1)S(1)} all-to-all(bf16[16,8,768]{2,1,0:T(8,128)(2,1)S(1)} %project.1), channel_id=1, replica_groups={{15,0,1,2,3,4,5,6,7,8,9,10,11,12,13,14},{31,16,17,18,19,20,21,22,23,24,..., dimensions={0} | all-to-all | bytes 393216 | tf_op jit(solution)/shard_map/all_to_all | solution.py:389
  25.1 0.1 convolution_convert_fusion
  25.3 0.1 broadcast_in_dim.8
  25.4 13.5 %all_to_all.16.own_ref = bf16[64,2,768]{2,1,0:T(2,128)(2,1)S(1)} all-to-all(bf16[64,2,768]{2,1,0:T(2,128)(2,1)S(1)} %bitcast.17), channel_id=1, replica_groups={{111,96,97,98,99,100,101,102,103,104,105,106,107,108,109,110,15,0,1,2,3..., dimensions={0} | all-to-all | bytes 393216 | tf_op jit(solution)/shard_map/all_to_all | solution.py:405
  38.9 4.1 %collective-permute-start.4 = (bf16[64,2,768]{2,1,0:T(2,128)(2,1)S(1)}, bf16[64,2,768]{2,1,0:T(2,128)(2,1)S(1)}, u32[]{:S(2)}, u32[]{:S(2)}) collective-permute-start(bf16[64,2,768]{2,1,0:T(2,128)(2,1)S(1)} %all_to_all.16.own_ref), channel_id=1, source_target_pairs={{0,16},{16,0},{32,48},{48,32},{64,80},{80,64},{96,112},{112,96},{1... | collective-permute-start | bytes 589832 | tf_op jit(solution)/shard_map/ppermute | solution.py:419
  43.0 1.1 %collective-permute-done.4.partner_ref = bf16[64,2,768]{2,1,0:T(2,128)(2,1)S(1)} collective-permute-done((bf16[64,2,768]{2,1,0:T(2,128)(2,1)S(1)}, bf16[64,2,768]{2,1,0:T(2,128)(2,1)S(1)}, u32[]{:S(2)}, u32[]{:S(2)}) %collective-permute-start.4) | collective-permute-done | bytes 196640 | tf_op jit(solution)/shard_map/ppermute | solution.py:419
  44.1 8.2 %experts.1 = bf16[128,2,768]{2,1,0:T(2,128)(2,1)S(1)} custom-call(s32[1]{0:T(128)} %bitcast.5.core_ref, bf16[64,2,768]{2,1,0:T(2,128)(2,1)S(1)} %all_to_all.16.own_ref, bf16[64,2,768]{2,1,0:T(2,128)(2,1)S(1)} %collective-permute-done.4.partner_ref, f32[1,6144]{1,0:T(1,128)S(1)} %get-tuple-element.28.gain_ref, bf16[576,6144]{1,0:T(8,128)(2,1)} %bitcast.14, ...), custom_call_target="tpu_custom_call" | custom-call | flops 679477248 | bytes 21233664 | tf_op jit(solution)/shard_map/experts/pallas_call | solution.py:334
  52.3 19.1 %all_to_all.17 = bf16[128,2,768]{2,1,0:T(2,128)(2,1)S(1)} all-to-all(bf16[128,2,768]{2,1,0:T(2,128)(2,1)S(1)} %experts.1), channel_id=1, replica_groups={{15,0,1,2,3,4,5,6,7,8,9,10,11,12,13,14,31,16,17,18,19,20,21,22,23,24,25..., dimensions={0} | all-to-all | bytes 786432 | tf_op jit(solution)/shard_map/all_to_all | solution.py:425
  71.3 0.1 reshape.33
  71.5 0.2 fusion
  71.7 0.6 reshape.32
  (5 shorter events, 0.1 us)
Async XLA Ops:
  0.6 11.7 %copy-start = (bf16[512,768]{1,0:T(8,128)(2,1)S(1)}, bf16[512,768]{1,0:T(8,128)(2,1)}, u32[]{:S(2)}) copy-start(bf16[512,768]{1,0:T(8,128)(2,1)} %weights_ref.1) | copy-start | bytes 2359300
  3.1 2.3 %collective-permute-start = (bf16[16,512]{1,0:T(8,128)(2,1)S(1)}, bf16[16,512]{1,0:T(8,128)(2,1)S(1)}, u32[]{:S(2)}, u32[]{:S(2)}) collective-permute-start(bf16[16,512]{1,0:T(8,128)(2,1)S(1)} %get-tuple-element.17), channel_id=1, source_target_pairs={{0,16},{16,0},{32,48},{48,32},{64,80},{80,64},{96,112},{112,96},{1... | collective-permute-start | bytes 49160 | tf_op jit(solution)/shard_map/ppermute | solution.py:380
  5.4 5.4 %collective-permute-start.3 = (bf16[32,512]{1,0:T(8,128)(2,1)S(1)}, bf16[32,512]{1,0:T(8,128)(2,1)S(1)}, u32[]{:S(2)}, u32[]{:S(2)}) collective-permute-start(bf16[32,512]{1,0:T(8,128)(2,1)S(1)} %maximum_select_fusion.own_ref), channel_id=1, source_target_pairs={{0,64},{16,80},{32,96},{48,112},{64,0},{80,16},{96,32},{112,48},{1... | collective-permute-start | bytes 98312 | tf_op jit(solution)/shard_map/ppermute | solution.py:385
  8.3 4.0 %collective-permute-start.2 = (bf16[32,512]{1,0:T(8,128)(2,1)S(1)}, bf16[32,512]{1,0:T(8,128)(2,1)S(1)}, u32[]{:S(2)}, u32[]{:S(2)}) collective-permute-start(bf16[32,512]{1,0:T(8,128)(2,1)S(1)} %maximum_select_fusion.own_ref), channel_id=1, source_target_pairs={{0,96},{16,112},{32,64},{48,80},{64,32},{80,48},{96,0},{112,16},{1... | collective-permute-start | bytes 98312 | tf_op jit(solution)/shard_map/ppermute | solution.py:385
  9.2 3.1 %collective-permute-start.1 = (bf16[32,512]{1,0:T(8,128)(2,1)S(1)}, bf16[32,512]{1,0:T(8,128)(2,1)S(1)}, u32[]{:S(2)}, u32[]{:S(2)}) collective-permute-start(bf16[32,512]{1,0:T(8,128)(2,1)S(1)} %maximum_select_fusion.own_ref), channel_id=1, source_target_pairs={{0,32},{16,48},{32,0},{48,16},{64,96},{80,112},{96,64},{112,80},{1... | collective-permute-start | bytes 98312 | tf_op jit(solution)/shard_map/ppermute | solution.py:385
  38.9 5.2 %collective-permute-start.4 = (bf16[64,2,768]{2,1,0:T(2,128)(2,1)S(1)}, bf16[64,2,768]{2,1,0:T(2,128)(2,1)S(1)}, u32[]{:S(2)}, u32[]{:S(2)}) collective-permute-start(bf16[64,2,768]{2,1,0:T(2,128)(2,1)S(1)} %all_to_all.16.own_ref), channel_id=1, source_target_pairs={{0,16},{16,0},{32,48},{48,32},{64,80},{80,64},{96,112},{112,96},{1... | collective-permute-start | bytes 589832 | tf_op jit(solution)/shard_map/ppermute | solution.py:419

commit v5 on v4

--- a/solution.py
+++ b/solution.py
@@ -10,6 +10,7 @@
 LATE_HEAD = 15
 FIRST_HEAD = 15
 FIRST_PLACE = 3
+LEAD = 64
 HIDDEN_STEPS = 4
 DOWN_WIDTHS = (3, 3, 2)
 TOGETHER = 2
@@ -251,8 +252,35 @@
     )(states, left, right, faded_twice)
 
 
+def lead_kernel(gate_in, up_in, gate_first, up_first, sems):
+    lead = gate_first.shape[0]
+    copies = [
+        pltpu.make_async_copy(source.at[pl.ds(0, lead)], target, sems.at[index])
+        for index, (source, target) in enumerate(((gate_in, gate_first), (up_in, up_first)))
+    ]
+    for copy in copies:
+        copy.start()
+    for copy in copies:
+        copy.wait()
+
+
+def lead_rows(gate, up):
+    anywhere = pl.BlockSpec(memory_space=pl.ANY)
+    first = pltpu.VMEM((LEAD, gate.shape[1]), gate.dtype)
+    return pl.pallas_call(
+        lead_kernel,
+        out_shape=[first, first],
+        in_specs=[anywhere] * 2,
+        out_specs=[pl.BlockSpec(memory_space=pltpu.VMEM)] * 2,
+        scratch_shapes=[pltpu.SemaphoreType.DMA((2,))],
+        compiler_params=pltpu.CompilerParams(vmem_limit_bytes=16 * 2**20),
+        cost_estimate=pl.CostEstimate(flops=0, bytes_accessed=4 * LEAD * gate.shape[1], transcendentals=0),
+        name="lead_rows",
+    )(in_hbm(gate), in_hbm(up))
+
+
 def experts_kernel(
-    core_ref, own_ref, partner_ref, gain_ref, gate_in, up_in, down_in, out_ref,
+    core_ref, own_ref, partner_ref, gain_ref, gate_first, up_first, gate_in, up_in, down_in, out_ref,
     normed, gate_ref, up_ref, down_ref, activated, sems,
 ):
     hidden, width = gate_in.shape
@@ -261,7 +289,8 @@
     places = places_in_order(shards // 2)
     blocks = own_ref.shape[0] // len(places)
     rows = blocks * own_ref.shape[1]
-    tile = hidden // HIDDEN_STEPS
+    lead = gate_first.shape[0]
+    tile = (hidden - lead) // HIDDEN_STEPS
     steps = HIDDEN_STEPS + len(DOWN_WIDTHS)
 
     def down_shards(step):
@@ -270,7 +299,7 @@
 
     def copies(step):
         if step < HIDDEN_STEPS:
-            cut = pl.ds(step * tile, tile)
+            cut = pl.ds(lead + step * tile, tile)
             parts = [(gate_in.at[cut], gate_ref.at[cut]), (up_in.at[cut], up_ref.at[cut])]
         else:
             here = down_shards(step - HIDDEN_STEPS)
@@ -305,12 +334,16 @@
     for shard in range(shards):
         cut = slice(shard * columns, (shard + 1) * columns)
         normed[:, cut] = (normed[:, cut].astype(jnp.float32) * scale * gain_ref[:, cut]).astype(jnp.bfloat16)
+    def activate(gate_rows, up_rows, cut):
+        gate = lax.dot_general(gate_rows, normed[...], ROWS_CONTRACT, preferred_element_type=jnp.float32)
+        upward = lax.dot_general(up_rows, normed[...], ROWS_CONTRACT, preferred_element_type=jnp.float32)
+        activated[cut, :] = (gate / (1.0 + jnp.exp(-gate)) * upward).astype(jnp.bfloat16)
+
+    activate(gate_first[...], up_first[...], slice(0, lead))
     for step in range(HIDDEN_STEPS):
         finish(step)
-        cut = slice(step * tile, (step + 1) * tile)
-        gate = lax.dot_general(gate_ref[cut], normed[...], ROWS_CONTRACT, preferred_element_type=jnp.float32)
-        upward = lax.dot_general(up_ref[cut], normed[...], ROWS_CONTRACT, preferred_element_type=jnp.float32)
-        activated[cut, :] = (gate / (1.0 + jnp.exp(-gate)) * upward).astype(jnp.bfloat16)
+        cut = slice(lead + step * tile, lead + (step + 1) * tile)
+        activate(gate_ref[cut], up_ref[cut], cut)
     for step in range(len(DOWN_WIDTHS)):
         finish(HIDDEN_STEPS + step)
         for shard in down_shards(step):
@@ -325,7 +358,7 @@
             )
 
 
-def expert_rows(core, own, partner, gain, gate, up, down):
+def expert_rows(core, own, partner, gain, firsts, gate, up, down):
     hidden, width = gate.shape
     count, slots, columns = own.shape
     rows = 2 * count * slots * columns // width
@@ -334,7 +367,7 @@
     return pl.pallas_call(
         experts_kernel,
         out_shape=jax.ShapeDtypeStruct((2 * count, slots, columns), jnp.bfloat16),
-        in_specs=[pl.BlockSpec(memory_space=pltpu.SMEM), vmem, vmem, vmem, hbm, hbm, hbm],
+        in_specs=[pl.BlockSpec(memory_space=pltpu.SMEM)] + [vmem] * 5 + [hbm] * 3,
         out_specs=vmem,
         scratch_shapes=[
             pltpu.VMEM((rows, width), jnp.bfloat16),
@@ -347,7 +380,7 @@
         compiler_params=pltpu.CompilerParams(vmem_limit_bytes=48 * 2**20),
         cost_estimate=pl.CostEstimate(flops=6 * rows * hidden * width, bytes_accessed=6 * hidden * width, transcendentals=0),
         name="experts",
-    )(core, own, partner, gain, in_hbm(gate), in_hbm(up), in_hbm(down))
+    )(core, own, partner, gain, *firsts, in_hbm(gate), in_hbm(up), in_hbm(down))
 
 
 def body(
@@ -413,11 +446,13 @@
         ],
         tiled=True,
     )
+    own, gate_source, up_source = lax.optimization_barrier((own, expert_gate[0], expert_up[0]))
     outgoing = expert_rows(
         (place % 2).astype(jnp.int32).reshape(1),
         own,
         lax.ppermute(own, "grp", [(one, one ^ 1) for one in range(groups)]),
         gain,
+        lead_rows(gate_source, up_source),
         expert_gate[0],
         expert_up[0],
         expert_down[0],

time: 72.5 us -> 72.3 us (level)
  waiting for transfers between devices: 3.4 us -> 2.33 us
  Pallas kernels: 12.5 us -> 13.5 us
    pallas_call x0 -> x1, Pallas kernels: none -> 1.39 us  [lead_rows(): pl.pallas_call(lead_kernel, out_shape=[first, first], in_specs=[anywhere]...]
    ppermute x1, waiting for transfers between devices: 1.07 us -> 0.01 us  [body(): lax.ppermute(own, 'grp', [(one, one ^ 1) for one in range(groups)])]
  transfers between devices with their start and end apart: 5 -> 5, of which waited for: 3 -> 2; matrix products, arithmetic and copies ran while one was open for 0% -> 0% of each run, Pallas kernels for 2% -> 4%
where the time goes in v5:
time: 72.3 us; the launch traced here: 72 us
  blocking collectives  44.8 us (62%)
  Pallas kernels  13.5 us (19%)
  starting transfers between devices  9.37 us (13%)
  waiting for transfers between devices  2.33 us (3%)
  local copies, waits for them, and re-layouts  0.86 us (1%)
  between operations  0.75 us (1%)
    all_to_all x1, blocking collectives, body(): lax.all_to_all(outgoing, ('grp', 'head'), split_axis=0, concat_axis=0, ax...  18.8 us
    all_to_all x1, blocking collectives, body(): lax.all_to_all(jnp.broadcast_to(slot_rows, (groups // 2, experts, CAP, co...  13.5 us
    all_to_all x1, blocking collectives, body(): lax.all_to_all(partial_sums, 'head', split_axis=0, concat_axis=0, axis_in...  12.5 us
    pallas_call x1, Pallas kernels, expert_rows(): pl.pallas_call(experts_kernel, out_shape=jax.ShapeDtypeStruct((2 * count,...  7.83 us
    ppermute x1, starting transfers between devices, body(): lax.ppermute(own, 'grp', [(one, one ^ 1) for one in range(groups)])  4.11 us
    ppermute x3, starting transfers between devices, body(): lax.ppermute(pair, 'grp', [(one, one ^ 2 * step) for one in range(groups)])  3.76 us
    pallas_call x1, Pallas kernels, attend(): pl.pallas_call(attend_kernel, out_shape=[pltpu.VMEM((requests * positions...  2.42 us
    pallas_call x1, Pallas kernels, update(): pl.pallas_call(update_kernel, out_shape=pltpu.HBM(states.shape, jnp.float...  1.61 us
  transfers between devices with their start and end apart: 5, of which 2 were waited for; matrix products, arithmetic and copies ran while one was open for 0% of the time, Pallas kernels for 4%

profile of v5, /device:TPU:1, one launch (start us, length us, event | category | flops | bytes accessed | tf_op | source)
XLA Modules:
  0.0 72.0 jit_solution(7371055425366865618)
XLA Ops:
  0.6 0.0 copy-start
  0.6 2.4 %attend.1 = (bf16[16,512]{1,0:T(8,128)(2,1)S(1)}, bf16[32,8]{1,0:T(8,128)(2,1)S(1)}, f32[8,32]{1,0:T(8,128)S(1)}, f32[8,768]{1,0:T(8,128)S(1)}, f32[1,6144]{1,0:...) custom-call(bf16[8,2,512]{2,1,0:T(2,128)(2,1)} %query_in.1, ...), custom_call_target="tpu_custom_call" | custom-call | flops 10000000 | bytes 2097152 | tf_op jit(solution)/shard_map/attend/pallas_call | solution.py:161
  3.1 1.5 %collective-permute-start = (bf16[16,512]{1,0:T(8,128)(2,1)S(1)}, bf16[16,512]{1,0:T(8,128)(2,1)S(1)}, u32[]{:S(2)}, u32[]{:S(2)}) collective-permute-start(bf16[16,512]{1,0:T(8,128)(2,1)S(1)} %get-tuple-element.22), channel_id=1, source_target_pairs={{0,16},{16,0},{32,48},{48,32},{64,80},{80,64},{96,112},{112,96},{1... | collective-permute-start | bytes 49160 | tf_op jit(solution)/shard_map/ppermute | solution.py:413
  4.6 0.8 %collective-permute-done = bf16[16,512]{1,0:T(8,128)(2,1)S(1)} collective-permute-done((bf16[16,512]{1,0:T(8,128)(2,1)S(1)}, bf16[16,512]{1,0:T(8,128)(2,1)S(1)}, u32[]{:S(2)}, u32[]{:S(2)}) %collective-permute-start) | collective-permute-done | bytes 16416 | tf_op jit(solution)/shard_map/ppermute | solution.py:413
  5.4 2.9 %collective-permute-start.3 = (bf16[32,512]{1,0:T(8,128)(2,1)S(1)}, bf16[32,512]{1,0:T(8,128)(2,1)S(1)}, u32[]{:S(2)}, u32[]{:S(2)}) collective-permute-start(bf16[32,512]{1,0:T(8,128)(2,1)S(1)} %maximum_select_fusion.own_ref), channel_id=1, source_target_pairs={{0,64},{16,80},{32,96},{48,112},{64,0},{80,16},{96,32},{112,48},{1... | collective-permute-start | bytes 98312 | tf_op jit(solution)/shard_map/ppermute | solution.py:418
  8.3 0.9 %collective-permute-start.2 = (bf16[32,512]{1,0:T(8,128)(2,1)S(1)}, bf16[32,512]{1,0:T(8,128)(2,1)S(1)}, u32[]{:S(2)}, u32[]{:S(2)}) collective-permute-start(bf16[32,512]{1,0:T(8,128)(2,1)S(1)} %maximum_select_fusion.own_ref), channel_id=1, source_target_pairs={{0,96},{16,112},{32,64},{48,80},{64,32},{80,48},{96,0},{112,16},{1... | collective-permute-start | bytes 98312 | tf_op jit(solution)/shard_map/ppermute | solution.py:418
  9.2 0.0 collective-permute-start.1
  9.2 1.6 %update.1 = f32[8,4,128,128]{3,2,1,0:T(8,128)} custom-call(f32[8,4,128,128]{3,2,1,0:T(8,128)S(1)} %get-tuple-element.23.states_ref, f32[8,4,512]{2,1,0:T(4,128)S(1)} %get-tuple-element.24.left_ref, f32[8,4,512]{2,1,0:T(4,128)S(1)} %get-tuple-element.25.right_ref, f32[1,512]{1,0:T(1,128)S(1)} %get-tuple-element.26.faded_ref), custom_call_target="tpu_custom_call" | custom-call | flops 10000000 | bytes 2097152 | tf_op jit(solution)/shard_map/update/pallas_call | solution.py:243
  10.8 0.0 collective-permute-done.3.fourth_ref
  10.8 1.5 %collective-permute-done.2.third_ref = bf16[32,512]{1,0:T(8,128)(2,1)S(1)} collective-permute-done((bf16[32,512]{1,0:T(8,128)(2,1)S(1)}, bf16[32,512]{1,0:T(8,128)(2,1)S(1)}, u32[]{:S(2)}, u32[]{:S(2)}) %collective-permute-start.2) | collective-permute-done | bytes 32800 | tf_op jit(solution)/shard_map/ppermute | solution.py:418
  12.3 0.0 collective-permute-done.1.second_ref
  12.3 0.0 copy-done
  12.3 0.3 project.1
  12.6 12.5 %all_to_all.15 = bf16[16,8,768]{2,1,0:T(8,128)(2,1)S(1)} all-to-all(bf16[16,8,768]{2,1,0:T(8,128)(2,1)S(1)} %project.1), channel_id=1, replica_groups={{15,0,1,2,3,4,5,6,7,8,9,10,11,12,13,14},{31,16,17,18,19,20,21,22,23,24,..., dimensions={0} | all-to-all | bytes 393216 | tf_op jit(solution)/shard_map/all_to_all | solution.py:422
  25.1 0.1 convolution_convert_fusion
  25.3 0.1 broadcast_in_dim.8
  25.4 13.5 %all_to_all.16.own_ref = bf16[64,2,768]{2,1,0:T(2,128)(2,1)S(1)} all-to-all(bf16[64,2,768]{2,1,0:T(2,128)(2,1)S(1)} %bitcast.19), channel_id=1, replica_groups={{111,96,97,98,99,100,101,102,103,104,105,106,107,108,109,110,15,0,1,2,3..., dimensions={0} | all-to-all | bytes 393216 | tf_op jit(solution)/shard_map/all_to_all | solution.py:438
  38.9 4.1 %collective-permute-start.4 = (bf16[64,2,768]{2,1,0:T(2,128)(2,1)S(1)}, bf16[64,2,768]{2,1,0:T(2,128)(2,1)S(1)}, u32[]{:S(2)}, u32[]{:S(2)}) collective-permute-start(bf16[64,2,768]{2,1,0:T(2,128)(2,1)S(1)} %all_to_all.16.own_ref), channel_id=1, source_target_pairs={{0,16},{16,0},{32,48},{48,32},{64,80},{80,64},{96,112},{112,96},{1... | collective-permute-start | bytes 589832 | tf_op jit(solution)/shard_map/ppermute | solution.py:453
  43.0 1.4 %lead_rows.1 = (bf16[64,6144]{1,0:T(8,128)(2,1)S(1)}, bf16[64,6144]{1,0:T(8,128)(2,1)S(1)}) custom-call(bf16[576,6144]{1,0:T(8,128)(2,1)} %bitcast.14, bf16[576,6144]{1,0:T(8,128)(2,1)} %bitcast.16), custom_call_target="tpu_custom_call" | custom-call | bytes 1572864 | tf_op jit(solution)/shard_map/lead_rows/pallas_call | solution.py:270
  44.4 0.0 collective-permute-done.4.partner_ref
  44.4 7.8 %experts.1 = bf16[128,2,768]{2,1,0:T(2,128)(2,1)S(1)} custom-call(s32[1]{0:T(128)} %bitcast.5.core_ref, bf16[64,2,768]{2,1,0:T(2,128)(2,1)S(1)} %all_to_all.16.own_ref, bf16[64,2,768]{2,1,0:T(2,128)(2,1)S(1)} %collective-permute-done.4.partner_ref, f32[1,6144]{1,0:T(1,128)S(1)} %get-tuple-element.34.gain_ref, ...), custom_call_target="tpu_custom_call" | custom-call | flops 679477248 | bytes 21233664 | tf_op jit(solution)/shard_map/experts/pallas_call | solution.py:367
  52.3 18.8 %all_to_all.17 = bf16[128,2,768]{2,1,0:T(2,128)(2,1)S(1)} all-to-all(bf16[128,2,768]{2,1,0:T(2,128)(2,1)S(1)} %experts.1), channel_id=1, replica_groups={{15,0,1,2,3,4,5,6,7,8,9,10,11,12,13,14,31,16,17,18,19,20,21,22,23,24,25..., dimensions={0} | all-to-all | bytes 786432 | tf_op jit(solution)/shard_map/all_to_all | solution.py:460
  71.1 0.1 reshape.33
  71.3 0.2 fusion
  71.4 0.6 reshape.32
  (5 shorter events, 0.1 us)
Async XLA Ops:
  0.6 11.7 %copy-start = (bf16[512,768]{1,0:T(8,128)(2,1)S(1)}, bf16[512,768]{1,0:T(8,128)(2,1)}, u32[]{:S(2)}) copy-start(bf16[512,768]{1,0:T(8,128)(2,1)} %weights_ref.1) | copy-start | bytes 2359300
  3.1 2.3 %collective-permute-start = (bf16[16,512]{1,0:T(8,128)(2,1)S(1)}, bf16[16,512]{1,0:T(8,128)(2,1)S(1)}, u32[]{:S(2)}, u32[]{:S(2)}) collective-permute-start(bf16[16,512]{1,0:T(8,128)(2,1)S(1)} %get-tuple-element.22), channel_id=1, source_target_pairs={{0,16},{16,0},{32,48},{48,32},{64,80},{80,64},{96,112},{112,96},{1... | collective-permute-start | bytes 49160 | tf_op jit(solution)/shard_map/ppermute | solution.py:413
  5.4 5.4 %collective-permute-start.3 = (bf16[32,512]{1,0:T(8,128)(2,1)S(1)}, bf16[32,512]{1,0:T(8,128)(2,1)S(1)}, u32[]{:S(2)}, u32[]{:S(2)}) collective-permute-start(bf16[32,512]{1,0:T(8,128)(2,1)S(1)} %maximum_select_fusion.own_ref), channel_id=1, source_target_pairs={{0,64},{16,80},{32,96},{48,112},{64,0},{80,16},{96,32},{112,48},{1... | collective-permute-start | bytes 98312 | tf_op jit(solution)/shard_map/ppermute | solution.py:418
  8.3 4.0 %collective-permute-start.2 = (bf16[32,512]{1,0:T(8,128)(2,1)S(1)}, bf16[32,512]{1,0:T(8,128)(2,1)S(1)}, u32[]{:S(2)}, u32[]{:S(2)}) collective-permute-start(bf16[32,512]{1,0:T(8,128)(2,1)S(1)} %maximum_select_fusion.own_ref), channel_id=1, source_target_pairs={{0,96},{16,112},{32,64},{48,80},{64,32},{80,48},{96,0},{112,16},{1... | collective-permute-start | bytes 98312 | tf_op jit(solution)/shard_map/ppermute | solution.py:418
  9.2 3.1 %collective-permute-start.1 = (bf16[32,512]{1,0:T(8,128)(2,1)S(1)}, bf16[32,512]{1,0:T(8,128)(2,1)S(1)}, u32[]{:S(2)}, u32[]{:S(2)}) collective-permute-start(bf16[32,512]{1,0:T(8,128)(2,1)S(1)} %maximum_select_fusion.own_ref), channel_id=1, source_target_pairs={{0,32},{16,48},{32,0},{48,16},{64,96},{80,112},{96,64},{112,80},{1... | collective-permute-start | bytes 98312 | tf_op jit(solution)/shard_map/ppermute | solution.py:418
  38.9 5.5 %collective-permute-start.4 = (bf16[64,2,768]{2,1,0:T(2,128)(2,1)S(1)}, bf16[64,2,768]{2,1,0:T(2,128)(2,1)S(1)}, u32[]{:S(2)}, u32[]{:S(2)}) collective-permute-start(bf16[64,2,768]{2,1,0:T(2,128)(2,1)S(1)} %all_to_all.16.own_ref), channel_id=1, source_target_pairs={{0,16},{16,0},{32,48},{48,32},{64,80},{80,64},{96,112},{112,96},{1... | collective-permute-start | bytes 589832 | tf_op jit(solution)/shard_map/ppermute | solution.py:453
